TPU v7x, 256 devices: a whole 4x4x8 slice. The times are simulated.
256 devices in a mesh: particle: 16 (over x_hi, z), shard: 16 (over y, x_lo, core).
Axes of the slice: x: 4 (x_hi: 2, x_lo: 2; x = x_hi * 2 + x_lo), y: 4, z: 8, core: 2. Of those that a mesh axis runs over, the one named last changes fastest.
Arguments:
- hidden: bfloat16 [32, 1024, 2432], P('particle', 'shard'), may hold values from -6 to 6
- ancestors: int32 [32], replicated, may hold values from 0 to 31
- timestep: int32 [1], replicated, may hold values from 0 to 27
- mod_table: float32 [28, 3, 2432], replicated, may hold values from -4 to 4
- w_qkv: bfloat16 [2432, 3648], P('shard'), may hold values from -0.125 to 0.125
- w_out: bfloat16 [1216, 2432], P('shard'), may hold values from -0.15625 to 0.15625
- q_gain: float32 [64], replicated, may hold values from 0.7 to 12
- k_gain: float32 [64], replicated, may hold values from 0.7 to 12
- text_kv: bfloat16 [2, 333, 1216], replicated, may hold values from -6 to 6
Outputs:
- block_out: bfloat16 [32, 1024, 2432], P('particle', 'shard')
All inputs are finite; a program needn't handle non-finite values.
Results may differ from a plain program's by a relative error of at most 0.014.
The roundings to bfloat16 on the way count: a program that leaves them out, or rounds other values in their place, can miss the bound.
Values may be sent and summed in bfloat16 or wider, within the bound.
No kernel may reach another device: no remote copies, remote signals or barrier semaphores. Data moves between devices by JAX's collectives and lax.ppermute only.
A program may use at most 128 MiB of HBM per device.

v0:
```python
import jax
import jax.numpy as jnp
from jax import lax
from jax.sharding import PartitionSpec as P

HD = 64


def head_norm(values, gain):
    squares = jnp.mean(values * values, axis=-1, keepdims=True)
    return (values * lax.rsqrt(squares + 1e-06) * gain).astype(jnp.bfloat16)


def on_device(hidden, ancestors, timestep, mod_table, w_qkv, w_out, q_gain, k_gain, text_kv):
    part_count = hidden.shape[0]
    rows = hidden.shape[1]
    width = hidden.shape[2]
    first = lax.axis_index("particle") * part_count
    own_parents = lax.dynamic_slice_in_dim(ancestors, first, part_count)
    piece = lax.all_gather(hidden, "particle", axis=0, tiled=True)
    labels = jnp.arange(piece.shape[0], dtype=jnp.int32)
    selector = (own_parents[:, None] == labels[None, :]).astype(jnp.bfloat16)
    picked = jnp.einsum("pj,jrd->prd", selector, piece, preferred_element_type=jnp.float32).astype(
        jnp.bfloat16
    )
    step_count = mod_table.shape[0]
    onehot = (jnp.arange(step_count, dtype=jnp.int32) == timestep[0]).astype(jnp.float32)
    modulation = jnp.dot(
        onehot, mod_table.reshape(step_count, 3 * width), precision=lax.Precision.HIGHEST
    ).reshape(3, width)
    shift_row = modulation[0]
    scale_row = modulation[1]
    gate_row = modulation[2]
    floats = picked.astype(jnp.float32)
    center = jnp.mean(floats, axis=-1, keepdims=True)
    spread = jnp.mean((floats - center) ** 2, axis=-1, keepdims=True)
    normed = (floats - center) * lax.rsqrt(spread + 1e-06)
    modulated = (normed * (1.0 + scale_row) + shift_row).astype(jnp.bfloat16)
    columns_all = w_qkv.shape[1]
    inner = columns_all // 3
    heads = inner // HD
    features = modulated
    qkv = jnp.einsum(
        "prd,dc->prc",
        features,
        lax.all_gather(w_qkv, "shard", axis=0, tiled=True),
        preferred_element_type=jnp.float32,
    )
    query = head_norm(qkv[:, :, :inner].reshape(part_count, rows, heads, HD), q_gain)
    keys = head_norm(qkv[:, :, inner : 2 * inner].reshape(part_count, rows, heads, HD), k_gain)
    values = qkv[:, :, 2 * inner :].astype(jnp.bfloat16)
    keys_flat = keys.reshape(part_count, rows, inner)
    factor = 1.0 / jnp.sqrt(jnp.float32(HD))
    text_count = text_kv.shape[1]
    text_keys = text_kv[0].reshape(text_count, heads, HD)
    text_values = text_kv[1].reshape(text_count, heads, HD)
    text_scores = (
        jnp.einsum("prhd,khd->phrk", query, text_keys, preferred_element_type=jnp.float32) * factor
    )
    first_max = jnp.max(text_scores, axis=-1)
    text_powers = jnp.exp(text_scores - first_max[..., None])
    first_sum = jnp.sum(text_powers, axis=-1)
    first_out = jnp.einsum(
        "phrk,khd->phrd",
        text_powers.astype(jnp.bfloat16),
        text_values,
        preferred_element_type=jnp.float32,
    )
    running_sum = first_sum
    running_out = first_out
    key_block = lax.all_gather(keys_flat, "shard", axis=1, tiled=True).reshape(
        part_count, -1, heads, HD
    )
    value_block = lax.all_gather(values, "shard", axis=1, tiled=True).reshape(
        part_count, -1, heads, HD
    )
    scores = (
        jnp.einsum("prhd,pkhd->phrk", query, key_block, preferred_element_type=jnp.float32) * factor
    )
    newest = jnp.maximum(first_max, jnp.max(scores, axis=-1))
    fading = jnp.exp(first_max - newest)
    powers = jnp.exp(scores - newest[..., None])
    running_sum = running_sum * fading + jnp.sum(powers, axis=-1)
    running_out = running_out * fading[..., None] + jnp.einsum(
        "phrk,pkhd->phrd",
        powers.astype(jnp.bfloat16),
        value_block,
        preferred_element_type=jnp.float32,
    )
    mixed = running_out / running_sum[..., None]
    attended = (
        jnp.transpose(mixed, (0, 2, 1, 3)).reshape(part_count, rows, inner).astype(jnp.bfloat16)
    )
    features = attended
    projected = jnp.einsum(
        "pri,id->prd",
        features,
        lax.all_gather(w_out, "shard", axis=0, tiled=True),
        preferred_element_type=jnp.float32,
    )
    return (floats + gate_row * projected).astype(jnp.bfloat16)


def solution(mesh):
    placed = (
        P("particle", "shard", None),
        P(),
        P(),
        P(),
        P("shard", None),
        P("shard", None),
        P(),
        P(),
        P(),
    )
    return jax.shard_map(
        on_device,
        mesh=mesh,
        in_specs=placed,
        out_specs=P("particle", "shard", None),
        check_vma=False,
    )
```

profile of v0, /device:TPU:1, one launch (start us, length us, event | category | flops | bytes accessed | tf_op | source)
XLA Modules:
  0.0 428.3 jit_solution(10535884254250110864)
XLA Ops:
  8.8 1.7 copy.55
  12.1 152.6 %all-gather.7.cloned.1.call-done = bf16[32,64,2432]{2,1,0:T(8,128)(2,1)} async-done(((bf16[2,64,2432]{2,1,0:T(8,128)(2,1)}), bf16[32,64,2432]{2,1,0:T(8,128)(2,1)}) %all-gather.7.cloned.1.call-update) | async-done | bytes 9961488 | tf_op jit(solution)/shard_map/all_gather | solution.py:20
  164.8 14.8 %fusion.59 = (f32[2,64]{0,1:T(8,128)S(1)}, f32[2,64,2432]{2,0,1:T(2,128)S(1)}) fusion(bf16[32,64,2432]{2,1,0:T(8,128)(2,1)} %all-gather.7.cloned.1.call-done, s32[2]{0:T(128)S(1)} %dynamic_slice.3), kind=kOutput, calls=%fused_computation.64 | convolution fusion | flops 20856768 | bytes 11207176 | tf_op jit(solution)/shard_map/pj,jrd->prd/dot_general | solution.py:23
  180.4 1.9 add_convert_fusion
  182.3 82.2 %all-gather.9.cloned.1.call-done = bf16[2432,3648]{1,0:T(8,128)(2,1)} async-done(((bf16[152,3648]{1,0:T(8,128)(2,1)}), bf16[2432,3648]{1,0:T(8,128)(2,1)}) %all-gather.9.cloned.1.call-update) | async-done | bytes 17743888 | tf_op jit(solution)/shard_map/all_gather | solution.py:46
  264.5 9.1 %fusion = f32[2,64,3648]{2,1,0:T(8,128)S(1)} fusion(bf16[2432,3648]{1,0:T(8,128)(2,1)} %all-gather.9.cloned.1.call-done, bf16[2,64,2432]{2,0,1:T(2,128)(2,1)} %add_convert_fusion), kind=kOutput, calls=%fused_computation | convolution fusion | flops 2271215616 | bytes 20234240 | tf_op jit(solution)/shard_map/prd,dc->prc/dot_general | solution.py:43
  274.6 2.6 mul.123
  277.2 1.9 reduce_sum.61
  280.8 2.6 mul.125
  283.4 2.3 fusion.56
  286.7 5.8 %fusion.57 = (bf16[1,333,1216]{2,0,1:T(2,128)(2,1)S(1)}, bf16[1,333,1216]{2,0,1:T(2,128)(2,1)}) fusion(bf16[2,333,1216]{2,0,1:T(2,128)(2,1)} %param.17), kind=kLoop, calls=%fused_computation.62 | loop fusion | bytes 3239424 | tf_op jit(solution)/shard_map/slice | solution.py:56
  292.6 4.3 %copy.57 = bf16[1,333,1216]{1,2,0:T(8,128)(2,1)} copy(bf16[1,333,1216]{2,0,1:T(2,128)(2,1)} %get-tuple-element.12) | data formatting | bytes 1619712 | tf_op jit(solution)/shard_map/slice | solution.py:55
  296.9 2.9 copy.59
  299.8 12.1 %all-gather.15.cloned.1.call-done = bf16[16,76,2432]{2,1,0:T(8,128)(2,1)} async-done(((bf16[1,76,2432]{2,1,0:T(8,128)(2,1)}), bf16[16,76,2432]{2,1,0:T(8,128)(2,1)}) %all-gather.15.cloned.1.call-update) | async-done | bytes 5914640 | tf_op jit(solution)/shard_map/all_gather | solution.py:98
  311.9 8.1 %reshape.96 = bf16[1216,2432,1]{1,0,2:T(8,128)(2,1)} reshape(bf16[16,76,2432]{2,1,0:T(8,128)(2,1)} %all-gather.15.cloned.1.call-done) | data formatting | bytes 11829248
  323.1 1.8 copy-done
  326.2 30.3 %all-gather.11.cloned.1.call-done = bf16[2,1024,1216]{2,1,0:T(8,128)(2,1)} async-done(((bf16[2,64,1216]{2,1,0:T(8,128)(2,1)}), bf16[2,1024,1216]{2,1,0:T(8,128)(2,1)}) %all-gather.11.cloned.1.call-update) | async-done | bytes 4980752 | tf_op jit(solution)/shard_map/all_gather | solution.py:71
  356.5 7.8 %copy.60 = bf16[2,1024,1216]{1,2,0:T(8,128)(2,1)} copy(bf16[2,1024,1216]{2,1,0:T(8,128)(2,1)} %all-gather.11.cloned.1.call-done) | data formatting | bytes 9961472 | tf_op jit(solution)/shard_map/all_gather | solution.py:71
  364.3 3.9 multiply_reduce_fusion
  368.3 3.7 fusion.4
  372.0 28.0 %all-gather.13.cloned.1.call-done = bf16[2,1024,1216]{2,1,0:T(8,128)(2,1)} async-done(((bf16[2,64,1216]{2,1,0:T(8,128)(2,1)}), bf16[2,1024,1216]{2,1,0:T(8,128)(2,1)}) %all-gather.13.cloned.1.call-update) | async-done | bytes 4980752 | tf_op jit(solution)/shard_map/all_gather | solution.py:74
  400.0 7.9 %copy.65 = bf16[2,1024,1216]{1,2,0:T(8,128)(2,1)} copy(bf16[2,1024,1216]{2,1,0:T(8,128)(2,1)} %all-gather.13.cloned.1.call-done) | data formatting | bytes 9961472 | tf_op jit(solution)/shard_map/all_gather | solution.py:74
  408.0 5.5 %fusion.31 = f32[2,64,19,64]{3,1,0,2:T(8,128)S(1)} fusion(bf16[2,1024,19,64]{1,3,2,0:T(8,128)(2,1)} %bitcast.76, bf16[2,19,64,1024]{3,2,1,0:T(8,128)(2,1)} %get-tuple-element.8), kind=kOutput, calls=%fused_computation.26 | convolution fusion | flops 318767104 | bytes 10584064 | tf_op jit(solution)/shard_map/phrk,pkhd->phrd/dot_general | solution.py:84
  415.9 3.7 fusion.60
  (57 shorter events, 16.6 us)
Async XLA Ops:
  6.5 158.2 %all-gather.7.cloned.1.call-start = ((), (), s32[]{:S(2)}) async-start(), calls=%async_computation | async-start | bytes 10584064 | tf_op jit(solution)/shard_map/all_gather | solution.py:20
  7.3 257.2 %all-gather.9.cloned.1.call-start = ((), (), s32[]{:S(2)}) async-start(), calls=%async_computation.1 | async-start | bytes 19183616 | tf_op jit(solution)/shard_map/all_gather | solution.py:46
  8.0 3.5 copy-start.7
  8.0 3.6 copy-start.9
  8.0 303.9 %all-gather.15.cloned.1.call-start = ((), (), s32[]{:S(2)}) async-start(), calls=%async_computation.4 | async-start | bytes 6615040 | tf_op jit(solution)/shard_map/all_gather | solution.py:98
  8.8 347.7 %all-gather.11.cloned.1.call-start = ((), (), s32[]{:S(2)}) async-start(), calls=%async_computation.2 | async-start | bytes 5570560 | tf_op jit(solution)/shard_map/all_gather | solution.py:71
  285.7 114.4 %all-gather.13.cloned.1.call-start = ((), (), s32[]{:S(2)}) async-start(), calls=%async_computation.3 | async-start | bytes 5570560 | tf_op jit(solution)/shard_map/all_gather | solution.py:74
  299.8 20.2 %copy-start.5 = (f32[2,64,1216]{2,1,0:T(8,128)S(1)}, f32[2,64,1216]{2,1,0:T(8,128)}, u32[]{:S(2)}) copy-start(f32[2,64,1216]{2,1,0:T(8,128)} %get-tuple-element.9) | copy-start | bytes 1867780
  320.0 0.9 copy-start.8
  320.4 2.0 copy-start.4
  321.5 0.9 copy-start.2
  323.1 1.8 copy-start
  326.2 38.2 %copy-start.3 = (bf16[2,64,19,64]{3,2,1,0:T(8,128)(2,1)S(1)}, bf16[2,64,19,64]{3,2,1,0:T(8,128)(2,1)}, u32[]{:S(2)}) copy-start(bf16[2,64,19,64]{3,2,1,0:T(8,128)(2,1)} %copy-done.2) | copy-start | bytes 933892
  408.0 5.5 %copy-start.1 = (f32[19,2,64,333]{3,2,1,0:T(8,128)S(1)}, f32[19,2,64,333]{3,2,1,0:T(8,128)}, u32[]{:S(2)}) copy-start(f32[19,2,64,333]{3,2,1,0:T(8,128)} %copy-done) | copy-start | bytes 9718276
  408.0 5.5 %copy-start.6 = (bf16[1,333,1216]{1,2,0:T(8,128)(2,1)S(1)}, bf16[1,333,1216]{1,2,0:T(8,128)(2,1)}, u32[]{:S(2)}) copy-start(bf16[1,333,1216]{1,2,0:T(8,128)(2,1)} %copy.59) | copy-start | bytes 2429572
Sparse Core Ops, SparseCore 0:
  9.9 154.7 all-gather.6
  166.6 97.8 all-gather.8
  266.3 45.5 all-gather.14
  313.6 42.8 all-gather.10
  358.2 41.8 all-gather.12
where the time goes:
time: 429 us; the launch traced here: 428 us
  waiting for transfers between devices  307 us (72%)
  local copies, waits for them, and re-layouts  51.6 us (12%)
  matrix products  39.7 us (9%)
  other arithmetic  15.1 us (4%)
  between operations  14 us (3%)
    all_gather x1, waiting for transfers between devices, on_device(): piece = lax.all_gather(hidden, 'particle', axis=0, tiled=True)  153 us
    all_gather x1, waiting for transfers between devices, on_device(): lax.all_gather(w_qkv, 'shard', axis=0, tiled=True)  82.2 us
    all_gather x1, waiting for transfers between devices, on_device(): lax.all_gather(keys_flat, 'shard', axis=1, tiled=True)  30.3 us
    all_gather x1, waiting for transfers between devices, on_device(): lax.all_gather(values, 'shard', axis=1, tiled=True)  28 us
    dot_general x1, matrix products, on_device(): jnp.einsum('pj,jrd->prd', selector, piece, preferred_element_type=jnp.flo...  14.8 us
    unnamed x24, local copies, waits for them, and re-layouts  12.9 us
    all_gather x1, waiting for transfers between devices, on_device(): lax.all_gather(w_out, 'shard', axis=0, tiled=True)  12.1 us
    dot_general x1, matrix products, on_device(): jnp.einsum('prd,dc->prc', features, lax.all_gather(w_qkv, 'shard', axis=0...  9.06 us
  transfers between devices with their start and end apart: 5, of which 5 were waited for; matrix products, arithmetic and copies ran while one was open for 19% of the time, Pallas kernels for 0%

commit v1 on v0

v1 whole, which is shorter than its diff:
```python
import functools

import jax
import jax.numpy as jnp
import numpy as np
from jax import lax
from jax.experimental import pallas as pl
from jax.experimental.pallas import tpu as pltpu
from jax.sharding import Mesh, PartitionSpec as P

HD = 64
AXES = ("xh", "z", "y", "xl", "c")
SIZES = (2, 8, 4, 2, 2)
GROUP = ("xh", "z")
GROUPS = 16
Y = 4
G = 4
NH = 5
HC = NH * HD
RT = 16


def params(mib=16):
    return pltpu.CompilerParams(vmem_limit_bytes=mib * 1024 * 1024)


def whole():
    return pl.BlockSpec(memory_space=pltpu.VMEM)


def scalar():
    return pl.BlockSpec(memory_space=pltpu.SMEM)


def swap(x, axis):
    return lax.ppermute(x, axis, [(0, 1), (1, 0)])


def turn(x, axis, by):
    n = SIZES[AXES.index(axis)]
    return lax.ppermute(x, axis, [(i, (i + by) % n) for i in range(n)])


def pack_kernel(fw, x_ref, o_ref):
    parts, rows, _ = x_ref.shape
    bw = o_ref.shape[-1] // Y
    for p in range(parts):
        for i in range(rows // RT):
            for g in range(G):
                pieces = []
                for y in range(Y):
                    lo = (y * G + g) * fw
                    pieces.append(x_ref[p, i * RT : (i + 1) * RT, lo : lo + fw])
                    pieces.append(jnp.zeros((RT, bw - fw), x_ref.dtype))
                o_ref[G * i + g, p] = jnp.concatenate(pieces, axis=-1)


def restore_kernel(fw, x_ref, o_ref):
    parts, rows, _ = o_ref.shape
    bw = x_ref.shape[-1] // Y
    for p in range(parts):
        for i in range(rows // RT):
            row = [x_ref[G * i + g, p] for g in range(G)]
            pieces = [row[g][:, y * bw : y * bw + fw] for y in range(Y) for g in range(G)]
            o_ref[p, i * RT : (i + 1) * RT, :] = jnp.concatenate(pieces, axis=-1)


def pick_kernel(a_ref, x_ref, o_ref):
    def step(p, _):
        o_ref[p] = x_ref[a_ref[p]]
        return 0

    lax.fori_loop(0, x_ref.shape[0], step, 0, unroll=4)


def norm_kernel(width, s_ref, x_ref, m_ref, k_ref, keep_ref, send_ref):
    parts = x_ref.shape[1]
    count = keep_ref.shape[1] // RT
    side = s_ref[0]
    live = k_ref[...]
    for which, o_ref in enumerate((keep_ref, send_ref)):
        for i in range(count):
            floats = [x_ref[G * i + g, side ^ which].astype(jnp.float32) for g in range(G)]
            center = sum(jnp.sum(f, axis=-1, keepdims=True) for f in floats) / width
            moved = [(f - center) * live for f in floats]
            spread = sum(jnp.sum(m * m, axis=-1, keepdims=True) for m in moved) / width
            inverse = lax.rsqrt(spread + 1e-06)
            for g in range(G):
                out = (moved[g] * inverse) * (1.0 + m_ref[1, g : g + 1]) + m_ref[0, g : g + 1]
                o_ref[g, i * RT : (i + 1) * RT, :] = out.astype(jnp.bfloat16)


def weight_kernel(s_ref, w_ref, o_ref):
    inner = w_ref.shape[1] // 3
    for y in range(Y):
        at = (y - s_ref[0]) & 3
        pieces = []
        for t in range(3):
            lo, hi = y * HC, min(inner, (y + 1) * HC)
            pieces.append(w_ref[:, t * inner + lo : t * inner + hi])
            if hi - lo < HC:
                pieces.append(jnp.zeros((w_ref.shape[0], HC - hi + lo), w_ref.dtype))
        o_ref[at] = jnp.concatenate(pieces, axis=-1)


def place_kernel(order, s_ref, *refs):
    *pieces, o_ref = refs
    for k, piece in enumerate(pieces):
        o_ref[order(k, s_ref)] = piece[...]


def placed_in_order(order, scalars, pieces):
    count = len(pieces)
    return pl.pallas_call(
        functools.partial(place_kernel, order),
        out_shape=jax.ShapeDtypeStruct((count,) + pieces[0].shape, pieces[0].dtype),
        in_specs=[scalar()] + [whole()] * count,
        out_specs=whole(),
        compiler_params=params(),
    )(scalars, *pieces)


def qkv_kernel(s_ref, *refs):
    x_refs, w_refs = refs[:4], refs[4:8]
    qg_ref, kg_ref, q_ref, kv_ref, x_buf, w_buf, sems = refs[8:]
    own = s_ref[0]
    rows, gw = x_refs[0].shape[1:]
    copies = [
        pltpu.make_async_copy(w_ref, w_buf.at[own ^ flip], sems.at[flip])
        for flip, w_ref in enumerate(w_refs)
    ]
    for copy in copies:
        copy.start()
    for k, x_ref in enumerate(x_refs):
        for g in range(G):
            x_buf[k * rows : (k + 1) * rows, g * gw : (g + 1) * gw] = x_ref[g]
    for copy in copies:
        copy.wait()
    acc = jnp.dot(
        x_buf[...], w_buf[...].reshape(G * gw, 3 * HC), preferred_element_type=jnp.float32
    )

    def normed(h, gain):
        v = acc[:, h * HD : (h + 1) * HD]
        ms = jnp.mean(v * v, axis=-1, keepdims=True)
        return (v * lax.rsqrt(ms + 1e-06) * gain).astype(jnp.bfloat16)

    for h in range(NH):
        q_ref[:, h * HD : (h + 1) * HD] = normed(h, qg_ref[...]) * jnp.bfloat16(0.125)
        kv_ref[:, h * HD : (h + 1) * HD] = normed(NH + h, kg_ref[...])
    kv_ref[:, HC:] = acc[:, 2 * HC :].astype(jnp.bfloat16)


def attention_kernel(text_count, s_ref, qa_ref, qb_ref, *refs):
    *sources, o_ref, k_buf, v_buf = refs
    rows = o_ref.shape[1]
    step = pl.program_id(0)

    @pl.when(step == 0)
    def _():
        at = 0
        for r in sources:
            span = slice(at, at + r.shape[0])
            at += r.shape[0]
            for h in range(NH):
                k_buf[h, span] = r[:, h * HD : (h + 1) * HD]
                v_buf[h, span] = r[:, HC + h * HD : HC + (h + 1) * HD]

    keys = k_buf.shape[1]
    cut = keys - 128
    live = cut + lax.broadcasted_iota(jnp.int32, (1, 128), 1) < keys - sources[-1].shape[0] + text_count
    heads = []
    for h in range(NH):
        ks = slice(h * HD, (h + 1) * HD)
        q = jnp.where(step == 0, qa_ref[:, ks], qb_ref[:, ks])

        def scored(span):
            return lax.dot_general(
                q, k_buf[h, span], (((1,), (1,)), ((), ())), preferred_element_type=jnp.float32
            )

        head, tail = scored(slice(0, cut)), jnp.where(live, scored(slice(cut, keys)), -jnp.inf)
        top = jnp.maximum(
            jnp.max(head, axis=-1, keepdims=True), jnp.max(tail, axis=-1, keepdims=True)
        )
        head, tail = jnp.exp(head - top), jnp.exp(tail - top)
        total = jnp.sum(head, axis=-1, keepdims=True) + jnp.sum(tail, axis=-1, keepdims=True)
        probs = jnp.concatenate([head.astype(jnp.bfloat16), tail.astype(jnp.bfloat16)], axis=-1)
        mixed = jnp.dot(probs, v_buf[h], preferred_element_type=jnp.float32)
        heads.append((mixed / total).astype(jnp.bfloat16))
    out = jnp.concatenate(heads, axis=-1)
    for k in range(Y):
        y = (s_ref[0] + k) & 3
        o_ref[2 * y + (s_ref[1] ^ step)] = out[k * rows : (k + 1) * rows]


def out_kernel(fo, s_ref, h_ref, wa_ref, wb_ref, x_ref, m_ref, o_ref, h_buf, w_buf, sems):
    parts, rows, width = o_ref.shape
    own = s_ref[0]
    copies = [
        pltpu.make_async_copy(wa_ref, w_buf.at[own], sems.at[0]),
        pltpu.make_async_copy(wb_ref, w_buf.at[1 - own], sems.at[1]),
    ]
    for copy in copies:
        copy.start()
    bo = wa_ref.shape[1]
    half = 2 * Y * bo
    for p in range(parts):
        row = jnp.concatenate([h_ref[2 * y + p] for y in range(Y)], axis=-1)
        for c in range(2):
            pieces = []
            for pair in range(2 * Y):
                s = 2 * pair + c
                pieces.append(row[:, s * fo : (s + 1) * fo])
                pieces.append(jnp.zeros((rows, bo - fo), row.dtype))
            h_buf[p * rows : (p + 1) * rows, c * half : (c + 1) * half] = jnp.concatenate(
                pieces, axis=-1
            )
    for copy in copies:
        copy.wait()
    acc = jnp.dot(
        h_buf[...], w_buf[...].reshape(2 * half, width), preferred_element_type=jnp.float32
    )
    gate = m_ref[...]
    for p in range(parts):
        floats = x_ref[p].astype(jnp.float32)
        o_ref[p] = (floats + gate * acc[p * rows : (p + 1) * rows]).astype(jnp.bfloat16)


def on_device(hidden, ancestors, timestep, mod_table, w_qkv, w_out, q_gain, k_gain, text_kv):
    parts, rows, width = hidden.shape
    inner = w_out.shape[0] * 16
    fw = w_qkv.shape[0]
    bw = -(-fw // 32) * 32
    gw = Y * bw
    yi, xi, ci = (lax.axis_index(a).astype(jnp.int32) for a in ("y", "xl", "c"))
    bf16 = jnp.bfloat16
    shape = jax.ShapeDtypeStruct

    packed = pl.pallas_call(
        functools.partial(pack_kernel, fw),
        out_shape=shape((GROUPS, parts, RT, gw), bf16),
        in_specs=[whole()],
        out_specs=whole(),
        compiler_params=params(),
    )(hidden)
    chunks = lax.all_to_all(packed, GROUP, 0, 0)

    w_qkv, packed_too = lax.optimization_barrier((w_qkv, packed))
    split = pl.pallas_call(
        weight_kernel,
        out_shape=shape((Y, bw, 3 * HC), bf16),
        in_specs=[scalar(), whole()],
        out_specs=whole(),
        compiler_params=params(),
    )(yi[None], jnp.pad(w_qkv, ((0, bw - fw), (0, 0))))
    w_mine = placed_in_order(
        lambda k, s: (s[0] - k) & 3, yi[None], [split[0]] + [turn(split[k], "y", k) for k in (1, 2, 3)]
    )
    fo = w_out.shape[0]
    w_out, w_mine = lax.optimization_barrier((w_out, w_mine))
    w_across = swap(w_mine, "c")
    w_side = swap(w_mine, "xl")
    w_corner = swap(w_side, "c")
    o_near = jnp.pad(w_out, ((0, -fo % RT), (0, 0)))
    o_side = swap(o_near, "xl")
    o_pieces = [p if k == 0 else turn(p, "y", -k) for p in (o_near, o_side) for k in range(Y)]
    o_mine = placed_in_order(
        lambda k, s: 2 * ((s[0] + k) & 3) + (s[1] ^ (k >> 2)), jnp.stack([yi, xi]), o_pieces
    )
    o_across = swap(o_mine, "c")

    text_count = text_kv.shape[1]
    text_pad = -(-text_count // 128) * 128
    text = jnp.pad(text_kv, ((0, 0), (0, text_pad - text_count), (0, Y * HC - inner)))
    text = lax.dynamic_slice_in_dim(text, yi * HC, HC, axis=2)
    text = jnp.concatenate([text[0], text[1]], axis=-1)

    modulation = lax.dynamic_index_in_dim(mod_table, timestep[0], 0, keepdims=False)
    gate = modulation[2:]
    modulation = modulation[:2]
    modulation = jnp.pad(modulation.reshape(2, Y, G, fw), ((0, 0), (0, 0), (0, 0), (0, bw - fw)))
    modulation = jnp.transpose(modulation, (0, 2, 1, 3)).reshape(2, G, gw)
    live = jnp.asarray((np.arange(gw) % bw < fw)[None], jnp.float32)
    live, modulation, gate, text, chunks = lax.optimization_barrier(
        (live, modulation, gate, text, chunks)
    )

    chosen = pl.pallas_call(
        pick_kernel,
        out_shape=shape((GROUPS * parts, RT, gw), bf16),
        in_specs=[scalar(), whole()],
        out_specs=whole(),
        compiler_params=params(),
    )(ancestors, chunks.reshape(GROUPS * parts, RT, gw))
    back = lax.all_to_all(chosen.reshape(GROUPS, parts, RT, gw), GROUP, 0, 0)

    keep, send = pl.pallas_call(
        functools.partial(norm_kernel, width),
        out_shape=[shape((G, rows, gw), bf16)] * 2,
        in_specs=[scalar()] + [whole()] * 3,
        out_specs=[whole()] * 2,
        compiler_params=params(),
    )(xi[None], back, modulation, live)

    def project(mine):
        blocks = [mine] + [turn(mine, "y", -k) for k in (1, 2, 3)]
        return pl.pallas_call(
            qkv_kernel,
            in_specs=[scalar()]
            + [whole()] * 4
            + [pl.BlockSpec(memory_space=pl.ANY)] * 4
            + [whole()] * 2,
            out_specs=[whole()] * 2,
            out_shape=[shape((Y * rows, HC), bf16), shape((Y * rows, 2 * HC), bf16)],
            scratch_shapes=[
                pltpu.VMEM((Y * rows, G * gw), bf16),
                pltpu.VMEM((G, Y, bw, 3 * HC), bf16),
                pltpu.SemaphoreType.DMA((G,)),
            ],
            compiler_params=params(32),
        )(
            (xi * 2 + ci)[None],
            *blocks,
            w_mine,
            w_across,
            w_side,
            w_corner,
            q_gain[None],
            k_gain[None],
        )

    q_a, kv_a = project(keep)
    q_b, kv_b = project(swap(send, "xl"))
    picked = pl.pallas_call(
        functools.partial(restore_kernel, fw),
        out_shape=shape((parts, rows, width), bf16),
        in_specs=[whole()],
        out_specs=whole(),
        compiler_params=params(),
    )(back)
    kv_c, kv_d = swap(kv_a, "c"), swap(kv_b, "c")
    count = q_a.shape[0]
    once = lambda r, w: pl.BlockSpec((r, w), lambda i: (0, 0))
    attended = pl.pallas_call(
        functools.partial(attention_kernel, text_count),
        grid=(2,),
        in_specs=[scalar()]
        + [once(count, HC)] * 2
        + [once(count, 2 * HC)] * 4
        + [once(text_pad, 2 * HC)],
        out_specs=pl.BlockSpec((2 * Y, rows, HC), lambda i: (0, 0, 0)),
        out_shape=shape((2 * Y, rows, HC), bf16),
        scratch_shapes=[pltpu.VMEM((NH, 4 * count + text_pad, HD), bf16)] * 2,
        compiler_params=params(40),
    )(jnp.stack([yi, xi]), q_a, q_b, kv_a, kv_b, kv_c, kv_d, text)

    home = lax.all_to_all(attended, ("y", "xl"), 0, 0)
    return pl.pallas_call(
        functools.partial(out_kernel, fo),
        in_specs=[scalar(), whole()]
        + [pl.BlockSpec(memory_space=pl.ANY)] * 2
        + [whole()] * 2,
        out_specs=whole(),
        out_shape=shape((parts, rows, width), bf16),
        scratch_shapes=[
            pltpu.VMEM((parts * rows, 2 * o_mine.size // width), bf16),
            pltpu.VMEM((2,) + o_mine.shape, bf16),
            pltpu.SemaphoreType.DMA((2,)),
        ],
        compiler_params=params(32),
    )(ci[None], home, o_mine, o_across, picked, gate)


def solution(mesh):
    fine = Mesh(np.asarray(mesh.devices).reshape(SIZES), AXES)
    placed = (
        P(("xh", "z"), ("y", "xl", "c"), None),
        P(),
        P(),
        P(),
        P(("y", "xl", "c"), None),
        P(("y", "xl", "c"), None),
        P(),
        P(),
        P(),
    )
    return jax.shard_map(
        on_device,
        mesh=fine,
        in_specs=placed,
        out_specs=P(("xh", "z"), ("y", "xl", "c"), None),
        check_vma=False,
    )
```

time: 429 us -> 176 us (0.41)
  waiting for transfers between devices: 307 us -> 71.5 us
  starting transfers between devices: 0.38 us -> 55 us
  local copies, waits for them, and re-layouts: 51.6 us -> 10.3 us
  matrix products: 39.7 us -> 0 us
  Pallas kernels: 0 us -> 36.8 us
  other arithmetic: 15.1 us -> 0.23 us
  between operations: 14 us -> 1.01 us
    all_gather x5 -> x0, waiting for transfers between devices: 305 us -> none  [the longest x1 153 us: on_device(): piece = lax.all_gather(hidden, 'particle', axis=0, tiled=True)]
    ppermute x0 -> x23, waiting for transfers between devices: none -> 45.5 us  [the longest x15 39.9 us: turn(): return lax.ppermute(x, axis, [(i, (i + by) % n) for i in range(n)])]
    dot_general x8 -> x0, matrix products: 39.7 us -> none  [the longest x1 14.8 us: on_device(): jnp.einsum('pj,jrd->prd', selector, piece, preferred_element_type=jnp.flo...]
    pallas_call x0 -> x11, Pallas kernels: none -> 36.8 us  [the longest x2 14.7 us: project(): pl.pallas_call(qkv_kernel, in_specs=[scalar()] + [whole()] * 4 + [pl.Bloc...]
    ppermute x0 -> x23, starting transfers between devices: none -> 31.7 us  [the longest x15 23.1 us: turn(): return lax.ppermute(x, axis, [(i, (i + by) % n) for i in range(n)])]
    all_to_all x0 -> x3, waiting for transfers between devices: none -> 26 us  [the longest x1 18 us: on_device(): back = lax.all_to_all(chosen.reshape(GROUPS, parts, RT, gw), GROUP, 0, 0)]
    all_to_all x0 -> x3, starting transfers between devices: none -> 23.4 us  [the longest x1 10.5 us: on_device(): chunks = lax.all_to_all(packed, GROUP, 0, 0)]
    all_gather x2 -> x0, local copies, waits for them, and re-layouts: 15.7 us -> none  [the longest x1 7.91 us: on_device(): lax.all_gather(values, 'shard', axis=1, tiled=True)]
  transfers between devices with their start and end apart: 5 -> 26, of which waited for: 5 -> 11; matrix products, arithmetic and copies ran while one was open for 19% -> 3% of each run, Pallas kernels for 0% -> 17%
where the time goes in v1:
time: 176 us; the launch traced here: 175 us
  waiting for transfers between devices  71.5 us (41%)
  starting transfers between devices  55 us (31%)
  Pallas kernels  36.8 us (21%)
  local copies, waits for them, and re-layouts  10.3 us (6%)
    ppermute x15, waiting for transfers between devices, turn(): return lax.ppermute(x, axis, [(i, (i + by) % n) for i in range(n)])  39.9 us
    ppermute x15, starting transfers between devices, turn(): return lax.ppermute(x, axis, [(i, (i + by) % n) for i in range(n)])  23.1 us
    all_to_all x1, waiting for transfers between devices, on_device(): back = lax.all_to_all(chosen.reshape(GROUPS, parts, RT, gw), GROUP, 0, 0)  18 us
    pallas_call x2, Pallas kernels, project(): pl.pallas_call(qkv_kernel, in_specs=[scalar()] + [whole()] * 4 + [pl.Bloc...  14.7 us
    all_to_all x1, starting transfers between devices, on_device(): chunks = lax.all_to_all(packed, GROUP, 0, 0)  10.5 us
    all_to_all x1, starting transfers between devices, on_device(): back = lax.all_to_all(chosen.reshape(GROUPS, parts, RT, gw), GROUP, 0, 0)  9.12 us
    pallas_call x1, Pallas kernels, on_device(): pl.pallas_call(functools.partial(attention_kernel, text_count), grid=(2,)...  8.98 us
    ppermute x8, starting transfers between devices, swap(): return lax.ppermute(x, axis, [(0, 1), (1, 0)])  8.59 us
  transfers between devices with their start and end apart: 26, of which 11 were waited for; matrix products, arithmetic and copies ran while one was open for 3% of the time, Pallas kernels for 17%

profile of v1, /device:TPU:1, one launch (start us, length us, event | category | flops | bytes accessed | tf_op | source)
XLA Modules:
  0.0 174.9 jit_solution(5695558189532247747)
XLA Ops:
  5.1 2.6 %collective-permute-start.4 = (bf16[160,960]{1,0:T(8,128)(2,1)S(1)}, bf16[160,960]{1,0:T(8,128)(2,1)S(1)}, u32[]{:S(2)}, u32[]{:S(2)}) collective-permute-start(bf16[160,960]{1,0:T(8,128)(2,1)S(1)} %get-tuple-element.36), channel_id=1, source_target_pairs={{0,8},{4,12},{8,0},{12,4},{1,9},{5,13},{9,1},{13,5},{2,10},{6,14},... | collective-permute-start | bytes 921608 | tf_op jit(solution)/shard_map/ppermute | solution.py:41
  8.8 3.1 %collective-permute-done.3.refs_1_ = bf16[160,960]{1,0:T(8,128)(2,1)S(1)} collective-permute-done((bf16[160,960]{1,0:T(8,128)(2,1)S(1)}, bf16[160,960]{1,0:T(8,128)(2,1)S(1)}, u32[]{:S(2)}, u32[]{:S(2)}) %collective-permute-start.3) | collective-permute-done | bytes 307232 | tf_op jit(solution)/shard_map/ppermute | solution.py:41
  11.9 9.9 %collective-permute-done.4.refs_2_ = bf16[160,960]{1,0:T(8,128)(2,1)S(1)} collective-permute-done((bf16[160,960]{1,0:T(8,128)(2,1)S(1)}, bf16[160,960]{1,0:T(8,128)(2,1)S(1)}, u32[]{:S(2)}, u32[]{:S(2)}) %collective-permute-start.4) | collective-permute-done | bytes 307232 | tf_op jit(solution)/shard_map/ppermute | solution.py:41
  24.1 2.9 %collective-permute-start.15 = (bf16[80,2432]{1,0:T(8,128)(2,1)S(1)}, bf16[80,2432]{1,0:T(8,128)(2,1)}, u32[]{:S(2)}, u32[]{:S(2)}) collective-permute-start(bf16[80,2432]{1,0:T(8,128)(2,1)S(1)} %pad.19.refs_0_), channel_id=1, source_target_pairs={{0,12},{4,0},{8,4},{12,8},{1,13},{5,1},{9,5},{13,9},{2,14},{6,2},{... | collective-permute-start | bytes 1167368 | tf_op jit(solution)/shard_map/ppermute | solution.py:41
  27.2 10.5 %all-to-all-start = ((bf16[16,2,16,640]{3,2,1,0:T(8,128)(2,1)}), bf16[16,2,16,640]{3,2,1,0:T(8,128)(2,1)S(1)}, u32[]{:S(2)}, u32[]{:S(2)}) async-start(bf16[16,2,16,640]{3,2,1,0:T(8,128)(2,1)} %shard_map.100), calls=%async_computation | async-start | bytes 1310720 | tf_op jit(solution)/shard_map/all_to_all | solution.py:247
  43.1 4.1 %collective-permute-done.17.refs_3_ = bf16[80,2432]{1,0:T(8,128)(2,1)} collective-permute-done((bf16[80,2432]{1,0:T(8,128)(2,1)S(1)}, bf16[80,2432]{1,0:T(8,128)(2,1)}, u32[]{:S(2)}, u32[]{:S(2)}) %collective-permute-start.17) | collective-permute-done | bytes 389152 | tf_op jit(solution)/shard_map/ppermute | solution.py:41
  47.2 5.9 %collective-permute-done.19.refs_5_ = bf16[80,2432]{1,0:T(8,128)(2,1)} collective-permute-done((bf16[80,2432]{1,0:T(8,128)(2,1)}, bf16[80,2432]{1,0:T(8,128)(2,1)}, u32[]{:S(2)}, u32[]{:S(2)}) %collective-permute-start.19) | collective-permute-done | bytes 389152 | tf_op jit(solution)/shard_map/ppermute | solution.py:41
  53.1 3.3 %collective-permute-done.20.refs_6_ = bf16[80,2432]{1,0:T(8,128)(2,1)} collective-permute-done((bf16[80,2432]{1,0:T(8,128)(2,1)}, bf16[80,2432]{1,0:T(8,128)(2,1)}, u32[]{:S(2)}, u32[]{:S(2)}) %collective-permute-start.20) | collective-permute-done | bytes 389152 | tf_op jit(solution)/shard_map/ppermute | solution.py:41
  56.4 7.5 %collective-permute-done.21.refs_7_ = bf16[80,2432]{1,0:T(8,128)(2,1)} collective-permute-done((bf16[80,2432]{1,0:T(8,128)(2,1)}, bf16[80,2432]{1,0:T(8,128)(2,1)}, u32[]{:S(2)}, u32[]{:S(2)}) %collective-permute-start.21) | collective-permute-done | bytes 389152 | tf_op jit(solution)/shard_map/ppermute | solution.py:41
  63.9 3.5 %shard_map.108.wa_ref = bf16[8,80,2432]{2,1,0:T(8,128)(2,1)} custom-call(s32[2]{0:T(128)S(1)} %pad_add_fusion.s_ref, bf16[80,2432]{1,0:T(8,128)(2,1)S(1)} %pad.19.refs_0_, bf16[80,2432]{1,0:T(8,128)(2,1)} %collective-permute-done.15.refs_1_, bf16[80,2432]{1,0:T(8,128)(2,1)} %collective-permute-done.16.refs_2_, ...), custom_call_target="tpu_custom_call" | custom-call | tf_op jit(solution)/shard_map/pallas_call | solution.py:114
  67.4 3.3 %collective-permute-start.22 = (bf16[8,80,2432]{2,1,0:T(8,128)(2,1)}, bf16[8,80,2432]{2,1,0:T(8,128)(2,1)}, u32[]{:S(2)}, u32[]{:S(2)}) collective-permute-start(bf16[8,80,2432]{2,1,0:T(8,128)(2,1)} %shard_map.108.wa_ref), channel_id=1, source_target_pairs={{0,1},{1,0},{2,3},{3,2},{4,5},{5,4},{6,7},{7,6},{8,9},{9,8},{10,11... | collective-permute-start | bytes 9338888 | tf_op jit(solution)/shard_map/ppermute | solution.py:36
  70.8 2.8 %copy.14 = bf16[2,333,1216]{2,1,0:T(8,128)(2,1)} copy(bf16[2,333,1216]{2,0,1:T(2,128)(2,1)} %param.18) | data formatting | bytes 3239424 | tf_op args[8]
  76.8 9.1 %all-to-all-start.1 = ((bf16[16,2,16,640]{3,2,1,0:T(8,128)(2,1)}), bf16[16,2,16,640]{3,2,1,0:T(8,128)(2,1)S(1)}, u32[]{:S(2)}, u32[]{:S(2)}) async-start(bf16[16,2,16,640]{3,2,1,0:T(8,128)(2,1)} %bitcast.10), calls=%async_computation.1 | async-start | bytes 1310720 | tf_op jit(solution)/shard_map/all_to_all | solution.py:296
  86.6 18.0 %all-to-all-done.1.x_ref = bf16[16,2,16,640]{3,2,1,0:T(8,128)(2,1)S(1)} async-done(((bf16[16,2,16,640]{3,2,1,0:T(8,128)(2,1)}), bf16[16,2,16,640]{3,2,1,0:T(8,128)(2,1)S(1)}, u32[]{:S(2)}, u32[]{:S(2)}) %all-to-all-start.1) | async-done | bytes 655392 | tf_op jit(solution)/shard_map/all_to_all | solution.py:296
  108.3 4.1 %collective-permute-done.9.refs_0_ = bf16[4,64,640]{2,1,0:T(8,128)(2,1)} collective-permute-done((bf16[4,64,640]{2,1,0:T(8,128)(2,1)S(1)}, bf16[4,64,640]{2,1,0:T(8,128)(2,1)}, u32[]{:S(2)}, u32[]{:S(2)}) %collective-permute-start.9) | collective-permute-done | bytes 327712 | tf_op jit(solution)/shard_map/ppermute | solution.py:36
  115.6 5.6 %collective-permute-start.12 = (bf16[4,64,640]{2,1,0:T(8,128)(2,1)}, bf16[4,64,640]{2,1,0:T(8,128)(2,1)}, u32[]{:S(2)}, u32[]{:S(2)}) collective-permute-start(bf16[4,64,640]{2,1,0:T(8,128)(2,1)} %collective-permute-done.9.refs_0_), channel_id=1, source_target_pairs={{0,4},{4,8},{8,12},{12,0},{1,5},{5,9},{9,13},{13,1},{2,6},{6,10},{... | collective-permute-start | bytes 983048 | tf_op jit(solution)/shard_map/ppermute | solution.py:41
  121.1 6.0 %collective-permute-done.2.refs_3_ = bf16[4,64,640]{2,1,0:T(8,128)(2,1)} collective-permute-done((bf16[4,64,640]{2,1,0:T(8,128)(2,1)}, bf16[4,64,640]{2,1,0:T(8,128)(2,1)}, u32[]{:S(2)}, u32[]{:S(2)}) %collective-permute-start.2) | collective-permute-done | bytes 327712 | tf_op jit(solution)/shard_map/ppermute | solution.py:41
  129.1 7.2 %shard_map.105 = (bf16[256,320]{1,0:T(8,128)(2,1)S(1)}, bf16[256,640]{1,0:T(8,128)(2,1)S(1)}) custom-call(s32[1]{0:T(128)} %bitcast.3.s_ref, bf16[4,64,640]{2,1,0:T(8,128)(2,1)} %get-tuple-element.22.refs_0_, bf16[4,64,640]{2,1,0:T(8,128)(2,1)S(1)} %copy-done.3, bf16[4,64,640]{2,1,0:T(8,128)(2,1)S(1)} %copy-done.5, ...), custom_call_target="tpu_custom_call" | custom-call | tf_op jit(solution)/shard_map/pallas_call | solution.py:308
  136.3 2.8 %collective-permute-start.13 = (bf16[256,640]{1,0:T(8,128)(2,1)S(1)}, bf16[256,640]{1,0:T(8,128)(2,1)S(1)}, u32[]{:S(2)}, u32[]{:S(2)}) collective-permute-start(bf16[256,640]{1,0:T(8,128)(2,1)S(1)} %get-tuple-element.28.refs_0_), channel_id=1, source_target_pairs={{0,1},{1,0},{2,3},{3,2},{4,5},{5,4},{6,7},{7,6},{8,9},{9,8},{10,11... | collective-permute-start | bytes 983048 | tf_op jit(solution)/shard_map/ppermute | solution.py:36
  139.2 7.4 %shard_map.106 = (bf16[256,320]{1,0:T(8,128)(2,1)S(1)}, bf16[256,640]{1,0:T(8,128)(2,1)S(1)}) custom-call(s32[1]{0:T(128)} %bitcast.3.s_ref, bf16[4,64,640]{2,1,0:T(8,128)(2,1)} %collective-permute-done.9.refs_0_, bf16[4,64,640]{2,1,0:T(8,128)(2,1)} %collective-permute-done.10.refs_1_, bf16[4,64,640]{2,1,0:T(8,128)(2,1)} %collective-permute-done.11.refs_2_, ...), custom_call_target="tpu_custom_call" | custom-call | tf_op jit(solution)/shard_map/pallas_call | solution.py:308
  148.6 9.0 %shard_map.107 = bf16[8,64,320]{2,1,0:T(8,128)(2,1)} custom-call(s32[2]{0:T(128)S(1)} %pad_add_fusion.s_ref, bf16[256,320]{1,0:T(8,128)(2,1)S(1)} %get-tuple-element.25.qa_ref, bf16[256,320]{1,0:T(8,128)(2,1)S(1)} %get-tuple-element.27.qb_ref, bf16[256,640]{1,0:T(8,128)(2,1)S(1)} %get-tuple-element.28.refs_0_, ...), custom_call_target="tpu_custom_call" | custom-call | tf_op jit(solution)/shard_map/pallas_call | solution.py:345
  157.5 3.8 %all-to-all-start.2 = ((bf16[8,64,320]{2,1,0:T(8,128)(2,1)}), bf16[8,64,320]{2,1,0:T(8,128)(2,1)S(1)}, u32[]{:S(2)}, u32[]{:S(2)}) async-start(bf16[8,64,320]{2,1,0:T(8,128)(2,1)} %shard_map.107), calls=%async_computation.2 | async-start | bytes 786432 | tf_op jit(solution)/shard_map/all_to_all | solution.py:358
  161.7 8.0 %all-to-all-done.2.h_ref = bf16[8,64,320]{2,1,0:T(8,128)(2,1)S(1)} async-done(((bf16[8,64,320]{2,1,0:T(8,128)(2,1)}), bf16[8,64,320]{2,1,0:T(8,128)(2,1)S(1)}, u32[]{:S(2)}, u32[]{:S(2)}) %all-to-all-start.2) | async-done | bytes 327712 | tf_op jit(solution)/shard_map/all_to_all | solution.py:358
  169.7 5.0 %shard_map.110 = bf16[2,64,2432]{2,1,0:T(8,128)(2,1)} custom-call(s32[1]{0:T(128)} %bitcast.s_ref, bf16[8,64,320]{2,1,0:T(8,128)(2,1)S(1)} %all-to-all-done.2.h_ref, bf16[8,80,2432]{2,1,0:T(8,128)(2,1)} %shard_map.108.wa_ref, bf16[8,80,2432]{2,1,0:T(8,128)(2,1)} %collective-permute-done.22.wb_ref, bf16[2,64,2432]{2,1,0:T(8,128)(2,1)S(1)} %shard_map.109.x_ref, ...), custom_call_target="tpu_custom_call" | custom-call | tf_op jit(solution)/shard_map/pallas_call | solution.py:359
  (76 shorter events, 28.2 us)
Async XLA Ops:
  2.9 9.0 %collective-permute-start.3 = (bf16[160,960]{1,0:T(8,128)(2,1)S(1)}, bf16[160,960]{1,0:T(8,128)(2,1)S(1)}, u32[]{:S(2)}, u32[]{:S(2)}) collective-permute-start(bf16[160,960]{1,0:T(8,128)(2,1)S(1)} %get-tuple-element.37), channel_id=1, source_target_pairs={{0,4},{4,8},{8,12},{12,0},{1,5},{5,9},{9,13},{13,1},{2,6},{6,10},{... | collective-permute-start | bytes 921608 | tf_op jit(solution)/shard_map/ppermute | solution.py:41
  5.1 16.8 %collective-permute-start.4 = (bf16[160,960]{1,0:T(8,128)(2,1)S(1)}, bf16[160,960]{1,0:T(8,128)(2,1)S(1)}, u32[]{:S(2)}, u32[]{:S(2)}) collective-permute-start(bf16[160,960]{1,0:T(8,128)(2,1)S(1)} %get-tuple-element.36), channel_id=1, source_target_pairs={{0,8},{4,12},{8,0},{12,4},{1,9},{5,13},{9,1},{13,5},{2,10},{6,14},... | collective-permute-start | bytes 921608 | tf_op jit(solution)/shard_map/ppermute | solution.py:41
  7.7 14.1 %collective-permute-start.5 = (bf16[160,960]{1,0:T(8,128)(2,1)S(1)}, bf16[160,960]{1,0:T(8,128)(2,1)S(1)}, u32[]{:S(2)}, u32[]{:S(2)}) collective-permute-start(bf16[160,960]{1,0:T(8,128)(2,1)S(1)} %get-tuple-element.35), channel_id=1, source_target_pairs={{0,12},{4,0},{8,4},{12,8},{1,13},{5,1},{9,5},{13,9},{2,14},{6,2},{... | collective-permute-start | bytes 921608 | tf_op jit(solution)/shard_map/ppermute | solution.py:41
  22.8 15.4 %collective-permute-start.18 = (bf16[80,2432]{1,0:T(8,128)(2,1)S(1)}, bf16[80,2432]{1,0:T(8,128)(2,1)}, u32[]{:S(2)}, u32[]{:S(2)}) collective-permute-start(bf16[80,2432]{1,0:T(8,128)(2,1)S(1)} %pad.19.refs_0_), channel_id=1, source_target_pairs={{0,2},{2,0},{1,3},{3,1},{4,6},{6,4},{5,7},{7,5},{8,10},{10,8},{9,1... | collective-permute-start | bytes 1167368 | tf_op jit(solution)/shard_map/ppermute | solution.py:36
  24.1 17.9 %collective-permute-start.15 = (bf16[80,2432]{1,0:T(8,128)(2,1)S(1)}, bf16[80,2432]{1,0:T(8,128)(2,1)}, u32[]{:S(2)}, u32[]{:S(2)}) collective-permute-start(bf16[80,2432]{1,0:T(8,128)(2,1)S(1)} %pad.19.refs_0_), channel_id=1, source_target_pairs={{0,12},{4,0},{8,4},{12,8},{1,13},{5,1},{9,5},{13,9},{2,14},{6,2},{... | collective-permute-start | bytes 1167368 | tf_op jit(solution)/shard_map/ppermute | solution.py:41
  27.1 15.0 %collective-permute-start.16 = (bf16[80,2432]{1,0:T(8,128)(2,1)S(1)}, bf16[80,2432]{1,0:T(8,128)(2,1)}, u32[]{:S(2)}, u32[]{:S(2)}) collective-permute-start(bf16[80,2432]{1,0:T(8,128)(2,1)S(1)} %pad.19.refs_0_), channel_id=1, source_target_pairs={{0,8},{4,12},{8,0},{12,4},{1,9},{5,13},{9,1},{13,5},{2,10},{6,14},... | collective-permute-start | bytes 1167368 | tf_op jit(solution)/shard_map/ppermute | solution.py:41
  27.2 48.1 %all-to-all-start = ((bf16[16,2,16,640]{3,2,1,0:T(8,128)(2,1)}), bf16[16,2,16,640]{3,2,1,0:T(8,128)(2,1)S(1)}, u32[]{:S(2)}, u32[]{:S(2)}) async-start(bf16[16,2,16,640]{3,2,1,0:T(8,128)(2,1)} %shard_map.100), calls=%async_computation | async-start | bytes 1310720 | tf_op jit(solution)/shard_map/all_to_all | solution.py:247
  37.7 9.5 %collective-permute-start.17 = (bf16[80,2432]{1,0:T(8,128)(2,1)S(1)}, bf16[80,2432]{1,0:T(8,128)(2,1)}, u32[]{:S(2)}, u32[]{:S(2)}) collective-permute-start(bf16[80,2432]{1,0:T(8,128)(2,1)S(1)} %pad.19.refs_0_), channel_id=1, source_target_pairs={{0,4},{4,8},{8,12},{12,0},{1,5},{5,9},{9,13},{13,1},{2,6},{6,10},{... | collective-permute-start | bytes 1167368 | tf_op jit(solution)/shard_map/ppermute | solution.py:41
  38.2 14.9 %collective-permute-start.19 = (bf16[80,2432]{1,0:T(8,128)(2,1)}, bf16[80,2432]{1,0:T(8,128)(2,1)}, u32[]{:S(2)}, u32[]{:S(2)}) collective-permute-start(bf16[80,2432]{1,0:T(8,128)(2,1)} %collective-permute-done.18.refs_4_), channel_id=1, source_target_pairs={{0,12},{4,0},{8,4},{12,8},{1,13},{5,1},{9,5},{13,9},{2,14},{6,2},{... | collective-permute-start | bytes 1167368 | tf_op jit(solution)/shard_map/ppermute | solution.py:41
  40.4 15.9 %collective-permute-start.20 = (bf16[80,2432]{1,0:T(8,128)(2,1)}, bf16[80,2432]{1,0:T(8,128)(2,1)}, u32[]{:S(2)}, u32[]{:S(2)}) collective-permute-start(bf16[80,2432]{1,0:T(8,128)(2,1)} %collective-permute-done.18.refs_4_), channel_id=1, source_target_pairs={{0,8},{4,12},{8,0},{12,4},{1,9},{5,13},{9,1},{13,5},{2,10},{6,14},... | collective-permute-start | bytes 1167368 | tf_op jit(solution)/shard_map/ppermute | solution.py:41
  42.1 21.8 %collective-permute-start.21 = (bf16[80,2432]{1,0:T(8,128)(2,1)}, bf16[80,2432]{1,0:T(8,128)(2,1)}, u32[]{:S(2)}, u32[]{:S(2)}) collective-permute-start(bf16[80,2432]{1,0:T(8,128)(2,1)} %collective-permute-done.18.refs_4_), channel_id=1, source_target_pairs={{0,4},{4,8},{8,12},{12,0},{1,5},{5,9},{9,13},{13,1},{2,6},{6,10},{... | collective-permute-start | bytes 1167368 | tf_op jit(solution)/shard_map/ppermute | solution.py:41
  42.1 44.2 %collective-permute-start.7 = (bf16[4,160,960]{2,1,0:T(8,128)(2,1)S(1)}, bf16[4,160,960]{2,1,0:T(8,128)(2,1)}, u32[]{:S(2)}, u32[]{:S(2)}) collective-permute-start(bf16[4,160,960]{2,1,0:T(8,128)(2,1)S(1)} %shard_map.104.refs_4_), channel_id=1, source_target_pairs={{0,2},{2,0},{1,3},{3,1},{4,6},{6,4},{5,7},{7,5},{8,10},{10,8},{9,1... | collective-permute-start | bytes 3686408 | tf_op jit(solution)/shard_map/ppermute | solution.py:36
  67.4 102.2 %collective-permute-start.22 = (bf16[8,80,2432]{2,1,0:T(8,128)(2,1)}, bf16[8,80,2432]{2,1,0:T(8,128)(2,1)}, u32[]{:S(2)}, u32[]{:S(2)}) collective-permute-start(bf16[8,80,2432]{2,1,0:T(8,128)(2,1)} %shard_map.108.wa_ref), channel_id=1, source_target_pairs={{0,1},{1,0},{2,3},{3,2},{4,5},{5,4},{6,7},{7,6},{8,9},{9,8},{10,11... | collective-permute-start | bytes 9338888 | tf_op jit(solution)/shard_map/ppermute | solution.py:36
  76.8 27.8 %all-to-all-start.1 = ((bf16[16,2,16,640]{3,2,1,0:T(8,128)(2,1)}), bf16[16,2,16,640]{3,2,1,0:T(8,128)(2,1)S(1)}, u32[]{:S(2)}, u32[]{:S(2)}) async-start(bf16[16,2,16,640]{3,2,1,0:T(8,128)(2,1)} %bitcast.10), calls=%async_computation.1 | async-start | bytes 1310720 | tf_op jit(solution)/shard_map/all_to_all | solution.py:296
  85.9 20.4 %collective-permute-start.6 = (bf16[4,160,960]{2,1,0:T(8,128)(2,1)S(1)}, bf16[4,160,960]{2,1,0:T(8,128)(2,1)}, u32[]{:S(2)}, u32[]{:S(2)}) collective-permute-start(bf16[4,160,960]{2,1,0:T(8,128)(2,1)S(1)} %shard_map.104.refs_4_), channel_id=1, source_target_pairs={{0,1},{1,0},{2,3},{3,2},{4,5},{5,4},{6,7},{7,6},{8,9},{9,8},{10,11... | collective-permute-start | bytes 3686408 | tf_op jit(solution)/shard_map/ppermute | solution.py:36
  86.3 21.2 %collective-permute-start.8 = (bf16[4,160,960]{2,1,0:T(8,128)(2,1)}, bf16[4,160,960]{2,1,0:T(8,128)(2,1)}, u32[]{:S(2)}, u32[]{:S(2)}) collective-permute-start(bf16[4,160,960]{2,1,0:T(8,128)(2,1)} %collective-permute-done.7.refs_6_), channel_id=1, source_target_pairs={{0,1},{1,0},{2,3},{3,2},{4,5},{5,4},{6,7},{7,6},{8,9},{9,8},{10,11... | collective-permute-start | bytes 3686408 | tf_op jit(solution)/shard_map/ppermute | solution.py:36
  105.8 7.1 %collective-permute-start = (bf16[4,64,640]{2,1,0:T(8,128)(2,1)}, bf16[4,64,640]{2,1,0:T(8,128)(2,1)S(1)}, u32[]{:S(2)}, u32[]{:S(2)}) collective-permute-start(bf16[4,64,640]{2,1,0:T(8,128)(2,1)} %get-tuple-element.22.refs_0_), channel_id=1, source_target_pairs={{0,12},{4,0},{8,4},{12,8},{1,13},{5,1},{9,5},{13,9},{2,14},{6,2},{... | collective-permute-start | bytes 983048 | tf_op jit(solution)/shard_map/ppermute | solution.py:41
  106.3 8.5 %collective-permute-start.1 = (bf16[4,64,640]{2,1,0:T(8,128)(2,1)}, bf16[4,64,640]{2,1,0:T(8,128)(2,1)S(1)}, u32[]{:S(2)}, u32[]{:S(2)}) collective-permute-start(bf16[4,64,640]{2,1,0:T(8,128)(2,1)} %get-tuple-element.22.refs_0_), channel_id=1, source_target_pairs={{0,8},{4,12},{8,0},{12,4},{1,9},{5,13},{9,1},{13,5},{2,10},{6,14},... | collective-permute-start | bytes 983048 | tf_op jit(solution)/shard_map/ppermute | solution.py:41
  107.5 19.6 %collective-permute-start.2 = (bf16[4,64,640]{2,1,0:T(8,128)(2,1)}, bf16[4,64,640]{2,1,0:T(8,128)(2,1)}, u32[]{:S(2)}, u32[]{:S(2)}) collective-permute-start(bf16[4,64,640]{2,1,0:T(8,128)(2,1)} %get-tuple-element.22.refs_0_), channel_id=1, source_target_pairs={{0,4},{4,8},{8,12},{12,0},{1,5},{5,9},{9,13},{13,1},{2,6},{6,10},{... | collective-permute-start | bytes 983048 | tf_op jit(solution)/shard_map/ppermute | solution.py:41
  112.4 26.8 %collective-permute-start.10 = (bf16[4,64,640]{2,1,0:T(8,128)(2,1)}, bf16[4,64,640]{2,1,0:T(8,128)(2,1)}, u32[]{:S(2)}, u32[]{:S(2)}) collective-permute-start(bf16[4,64,640]{2,1,0:T(8,128)(2,1)} %collective-permute-done.9.refs_0_), channel_id=1, source_target_pairs={{0,12},{4,0},{8,4},{12,8},{1,13},{5,1},{9,5},{13,9},{2,14},{6,2},{... | collective-permute-start | bytes 983048 | tf_op jit(solution)/shard_map/ppermute | solution.py:41
  113.7 25.5 %collective-permute-start.11 = (bf16[4,64,640]{2,1,0:T(8,128)(2,1)}, bf16[4,64,640]{2,1,0:T(8,128)(2,1)}, u32[]{:S(2)}, u32[]{:S(2)}) collective-permute-start(bf16[4,64,640]{2,1,0:T(8,128)(2,1)} %collective-permute-done.9.refs_0_), channel_id=1, source_target_pairs={{0,8},{4,12},{8,0},{12,4},{1,9},{5,13},{9,1},{13,5},{2,10},{6,14},... | collective-permute-start | bytes 983048 | tf_op jit(solution)/shard_map/ppermute | solution.py:41
  115.6 23.6 %collective-permute-start.12 = (bf16[4,64,640]{2,1,0:T(8,128)(2,1)}, bf16[4,64,640]{2,1,0:T(8,128)(2,1)}, u32[]{:S(2)}, u32[]{:S(2)}) collective-permute-start(bf16[4,64,640]{2,1,0:T(8,128)(2,1)} %collective-permute-done.9.refs_0_), channel_id=1, source_target_pairs={{0,4},{4,8},{8,12},{12,0},{1,5},{5,9},{9,13},{13,1},{2,6},{6,10},{... | collective-permute-start | bytes 983048 | tf_op jit(solution)/shard_map/ppermute | solution.py:41
  136.3 10.7 %collective-permute-start.13 = (bf16[256,640]{1,0:T(8,128)(2,1)S(1)}, bf16[256,640]{1,0:T(8,128)(2,1)S(1)}, u32[]{:S(2)}, u32[]{:S(2)}) collective-permute-start(bf16[256,640]{1,0:T(8,128)(2,1)S(1)} %get-tuple-element.28.refs_0_), channel_id=1, source_target_pairs={{0,1},{1,0},{2,3},{3,2},{4,5},{5,4},{6,7},{7,6},{8,9},{9,8},{10,11... | collective-permute-start | bytes 983048 | tf_op jit(solution)/shard_map/ppermute | solution.py:36
  157.5 12.1 %all-to-all-start.2 = ((bf16[8,64,320]{2,1,0:T(8,128)(2,1)}), bf16[8,64,320]{2,1,0:T(8,128)(2,1)S(1)}, u32[]{:S(2)}, u32[]{:S(2)}) async-start(bf16[8,64,320]{2,1,0:T(8,128)(2,1)} %shard_map.107), calls=%async_computation.2 | async-start | bytes 786432 | tf_op jit(solution)/shard_map/all_to_all | solution.py:358
  (14 other events, 189.8 us)

commit v2 on v1

v2 whole, which is shorter than its diff:
```python
import functools

import jax
import jax.numpy as jnp
import numpy as np
from jax import lax
from jax.experimental import pallas as pl
from jax.experimental.pallas import tpu as pltpu
from jax.sharding import Mesh, PartitionSpec as P

HD = 64
AXES = ("xh", "z", "y", "xl", "c")
SIZES = (2, 8, 4, 2, 2)
GROUP = ("xh", "z")
GROUPS = 16
Y = 4
G = 4
NH = 5
HC = NH * HD
RT = 16
FIRST = ((0, 0), (0, 1), (1, 0), (3, 0))
SECOND = ((1, 1), (3, 1), (2, 0), (2, 1))


def params(mib=16):
    return pltpu.CompilerParams(vmem_limit_bytes=mib * 1024 * 1024)


def whole():
    return pl.BlockSpec(memory_space=pltpu.VMEM)


def scalar():
    return pl.BlockSpec(memory_space=pltpu.SMEM)


def swap(x, axis):
    return lax.ppermute(x, axis, [(0, 1), (1, 0)])


def turn(x, axis, by):
    n = SIZES[AXES.index(axis)]
    return lax.ppermute(x, axis, [(i, (i + by) % n) for i in range(n)])


def beside(x, by):
    n = 4
    return lax.ppermute(x, ("xh", "xl"), [(i, (i + by) % n) for i in range(n)])


def across(x, by):
    pairs = [(2 * y + l, 2 * ((y + by) % Y) + 1 - l) for y in range(Y) for l in range(2)]
    return lax.ppermute(x, ("y", "xl"), pairs)


def pack_kernel(fw, x_ref, o_ref):
    parts, rows, _ = x_ref.shape
    bw = o_ref.shape[-1] // Y
    for p in range(parts):
        for i in range(rows // RT):
            for g in range(G):
                pieces = []
                for y in range(Y):
                    lo = (y * G + g) * fw
                    pieces.append(x_ref[p, i * RT : (i + 1) * RT, lo : lo + fw])
                    pieces.append(jnp.zeros((RT, bw - fw), x_ref.dtype))
                o_ref[G * i + g, p] = jnp.concatenate(pieces, axis=-1)


def restore_kernel(fw, x_ref, o_ref):
    parts, rows, _ = o_ref.shape
    bw = x_ref.shape[-1] // Y
    for p in range(parts):
        for i in range(rows // RT):
            row = [x_ref[G * i + g, p] for g in range(G)]
            pieces = [row[g][:, y * bw : y * bw + fw] for y in range(Y) for g in range(G)]
            o_ref[p, i * RT : (i + 1) * RT, :] = jnp.concatenate(pieces, axis=-1)


def pick_kernel(a_ref, x_ref, o_ref):
    def step(p, _):
        o_ref[p] = x_ref[a_ref[p]]
        return 0

    lax.fori_loop(0, x_ref.shape[0], step, 0, unroll=4)


def norm_kernel(fw, s_ref, x_ref, m_ref, keep_ref, send_ref):
    count = keep_ref.shape[1] // RT
    bw = keep_ref.shape[-1] // Y
    width = m_ref.shape[-1]
    side = s_ref[0]
    lane = lax.broadcasted_iota(jnp.int32, (1, Y * bw), 1)
    live = jnp.zeros((1, Y * bw), jnp.float32)
    for y in range(Y):
        live = jnp.where((lane >= y * bw) & (lane < y * bw + fw), 1.0, live)

    def grouped(row):
        out = []
        for g in range(G):
            pieces = []
            for y in range(Y):
                lo = (y * G + g) * fw
                pieces += [m_ref[row : row + 1, lo : lo + fw], jnp.zeros((1, bw - fw), jnp.float32)]
            out.append(jnp.concatenate(pieces, axis=-1))
        return out

    shift, scale = grouped(0), [1.0 + r for r in grouped(1)]
    for which, o_ref in enumerate((keep_ref, send_ref)):
        for i in range(count):
            floats = [x_ref[G * i + g, side ^ which].astype(jnp.float32) for g in range(G)]
            center = sum(jnp.sum(f, axis=-1, keepdims=True) for f in floats) / width
            moved = [(f - center) * live for f in floats]
            spread = sum(jnp.sum(m * m, axis=-1, keepdims=True) for m in moved) / width
            inverse = lax.rsqrt(spread + 1e-06)
            for g in range(G):
                out = (moved[g] * inverse) * scale[g] + shift[g]
                o_ref[g, i * RT : (i + 1) * RT, :] = out.astype(jnp.bfloat16)


def weight_kernel(s_ref, w_ref, o_ref):
    inner = w_ref.shape[1] // 3
    for y in range(Y):
        at = (y - s_ref[0]) & 3
        pieces = []
        for t in range(3):
            lo, hi = y * HC, min(inner, (y + 1) * HC)
            pieces.append(w_ref[:, t * inner + lo : t * inner + hi])
            if hi - lo < HC:
                pieces.append(jnp.zeros((w_ref.shape[0], HC - hi + lo), w_ref.dtype))
        o_ref[at] = jnp.concatenate(pieces, axis=-1)


def place_kernel(order, s_ref, *refs):
    *pieces, o_ref = refs
    for k, piece in enumerate(pieces):
        o_ref[order(k, s_ref)] = piece[...]


def join_kernel(*refs):
    *pieces, o_ref = refs
    at = 0
    for piece in pieces:
        o_ref[at : at + piece.shape[0]] = piece[...]
        at += piece.shape[0]


def placed_in_order(order, scalars, pieces):
    count = len(pieces)
    return pl.pallas_call(
        functools.partial(place_kernel, order),
        out_shape=jax.ShapeDtypeStruct((count,) + pieces[0].shape, pieces[0].dtype),
        in_specs=[scalar()] + [whole()] * count,
        out_specs=whole(),
        compiler_params=params(),
    )(scalars, *pieces)


def qkv_kernel(s_ref, *refs):
    x_refs = refs[:4]
    w_ref, qg_ref, kg_ref, q_ref, kv_ref, x_buf = refs[4:]
    rows, gw = x_refs[0].shape[1:]
    for k, x_ref in enumerate(x_refs):
        for flip in range(G):
            x_buf[k * rows : (k + 1) * rows, flip * gw : (flip + 1) * gw] = x_ref[s_ref[0] ^ flip]
    acc = jnp.dot(
        x_buf[...], w_ref[...].reshape(G * gw, 3 * HC), preferred_element_type=jnp.float32
    )

    def normed(h, gain):
        v = acc[:, h * HD : (h + 1) * HD]
        ms = jnp.mean(v * v, axis=-1, keepdims=True)
        return (v * lax.rsqrt(ms + 1e-06) * gain).astype(jnp.bfloat16)

    for h in range(NH):
        q_ref[:, h * HD : (h + 1) * HD] = normed(h, qg_ref[...]) * jnp.bfloat16(0.125)
        kv_ref[:, h * HD : (h + 1) * HD] = normed(NH + h, kg_ref[...])
    kv_ref[:, HC:] = acc[:, 2 * HC :].astype(jnp.bfloat16)


def attention_kernel(text_count, s_ref, *refs):
    given, (o_ref, q_buf, kv_buf, k_buf, v_buf, sems) = refs[:7], refs[7:]
    rows = o_ref.shape[1]
    step = pl.program_id(0)

    @pl.when(step == 0)
    def _():
        copies, spans, at = [], [], 0
        for k, r in enumerate(given):
            if k < 2:
                to = q_buf.at[k]
            else:
                spans.append(slice(at, at + r.shape[0]))
                at += r.shape[0]
                to = kv_buf.at[spans[-1]]
            copies.append(pltpu.make_async_copy(r, to, sems.at[k]))
        for copy in copies:
            copy.start()
        for copy, span in zip(copies[2:], spans):
            copy.wait()
            for h in range(NH):
                k_buf[h, span] = kv_buf[span, h * HD : (h + 1) * HD]
                v_buf[h, span] = kv_buf[span, HC + h * HD : HC + (h + 1) * HD]
        for copy in copies[:2]:
            copy.wait()

    keys = k_buf.shape[1]
    cut = keys - 128
    live = cut + lax.broadcasted_iota(jnp.int32, (1, 128), 1) < keys - given[-1].shape[0] + text_count
    heads = []
    for h in range(NH):
        ks = slice(h * HD, (h + 1) * HD)
        q = q_buf[step, :, ks]

        def scored(span):
            return lax.dot_general(
                q, k_buf[h, span], (((1,), (1,)), ((), ())), preferred_element_type=jnp.float32
            )

        head, tail = scored(slice(0, cut)), jnp.where(live, scored(slice(cut, keys)), -jnp.inf)
        top = jnp.maximum(
            jnp.max(head, axis=-1, keepdims=True), jnp.max(tail, axis=-1, keepdims=True)
        )
        head, tail = jnp.exp(head - top), jnp.exp(tail - top)
        total = jnp.sum(head, axis=-1, keepdims=True) + jnp.sum(tail, axis=-1, keepdims=True)
        probs = jnp.concatenate([head.astype(jnp.bfloat16), tail.astype(jnp.bfloat16)], axis=-1)
        mixed = jnp.dot(probs, v_buf[h], preferred_element_type=jnp.float32)
        heads.append((mixed / total).astype(jnp.bfloat16))
    out = jnp.concatenate(heads, axis=-1)
    for k in range(Y):
        (turn_a, flip_a), (turn_b, flip_b) = FIRST[k], SECOND[k]
        y = (s_ref[0] + jnp.where(step == 0, turn_a, turn_b)) & 3
        side = s_ref[1] ^ jnp.where(step == 0, flip_a, flip_b)
        o_ref[2 * y + side] = out[k * rows : (k + 1) * rows]


def out_kernel(fo, s_ref, h_ref, x_ref, m_ref, *refs):
    *given, o_ref, h_buf, w_buf, sems = refs
    parts, rows, width = o_ref.shape
    count, bo, _ = w_buf.shape
    copies, filled = [], 0
    for k, r in enumerate(given):
        to = w_buf.at[filled : filled + r.shape[0]]
        filled += r.shape[0]
        copies.append(pltpu.make_async_copy(r, to, sems.at[k]))
    for copy in copies:
        copy.start()
    for p in range(parts):
        row = jnp.concatenate([h_ref[2 * y + p] for y in range(Y)], axis=-1)
        for s in range(count):
            y, x, c = s // 4, s // 2 % 2, s % 2
            at = 4 * (c ^ s_ref[2]) + ((y - s_ref[0]) & 3)
            piece = [row[:, s * fo : (s + 1) * fo], jnp.zeros((rows, bo - fo), row.dtype)]
            h_buf[2 * at + (x ^ s_ref[1]), p * rows : (p + 1) * rows, :] = jnp.concatenate(
                piece, axis=-1
            )
    features = jnp.concatenate([h_buf[k] for k in range(count)], axis=-1)
    for copy in copies:
        copy.wait()
    acc = jnp.dot(
        features, w_buf[...].reshape(count * bo, width), preferred_element_type=jnp.float32
    )
    gate = m_ref[...]
    for p in range(parts):
        floats = x_ref[p].astype(jnp.float32)
        o_ref[p] = (floats + gate * acc[p * rows : (p + 1) * rows]).astype(jnp.bfloat16)


def on_device(hidden, ancestors, timestep, mod_table, w_qkv, w_out, q_gain, k_gain, text_kv):
    parts, rows, width = hidden.shape
    inner = w_out.shape[0] * 16
    fw = w_qkv.shape[0]
    bw = -(-fw // 32) * 32
    gw = Y * bw
    yi, xi, ci = (lax.axis_index(a).astype(jnp.int32) for a in ("y", "xl", "c"))
    bf16 = jnp.bfloat16
    shape = jax.ShapeDtypeStruct

    packed = pl.pallas_call(
        functools.partial(pack_kernel, fw),
        out_shape=shape((GROUPS, parts, RT, gw), bf16),
        in_specs=[whole()],
        out_specs=whole(),
        compiler_params=params(),
    )(hidden)
    chunks = lax.all_to_all(packed, GROUP, 0, 0)

    w_qkv, w_out, packed_too = lax.optimization_barrier((w_qkv, w_out, packed))
    split = pl.pallas_call(
        weight_kernel,
        out_shape=shape((Y, bw, 3 * HC), bf16),
        in_specs=[scalar(), whole()],
        out_specs=whole(),
        compiler_params=params(),
    )(yi[None], jnp.pad(w_qkv, ((0, bw - fw), (0, 0))))
    w_pieces = [split[0]] + [turn(split[k], "y", k) for k in (1, 2, 3)]
    fo = w_out.shape[0]
    o_near = jnp.pad(w_out, ((0, -fo % RT), (0, 0)))
    o_side = swap(o_near, "xl")

    chunks, w_pieces, o_side = lax.optimization_barrier((chunks, w_pieces, o_side))
    w_mine = placed_in_order(lambda k, s: (s[0] - k) & 3, yi[None], w_pieces)

    modulation = lax.dynamic_index_in_dim(mod_table, timestep[0], 0, keepdims=False)
    gate = modulation[2:]

    chosen = pl.pallas_call(
        pick_kernel,
        out_shape=shape((GROUPS * parts, RT, gw), bf16),
        in_specs=[scalar(), whole()],
        out_specs=whole(),
        compiler_params=params(),
    )(ancestors, chunks.reshape(GROUPS * parts, RT, gw))

    chosen, w_mine, o_near, o_side = lax.optimization_barrier((chosen, w_mine, o_near, o_side))
    back = lax.all_to_all(chosen.reshape(GROUPS, parts, RT, gw), GROUP, 0, 0)
    w_sides = [beside(w_mine[: Y // 2], 1), beside(w_mine[Y // 2 :], -1)]
    w_across = swap(w_mine, "c")
    o_own = jnp.stack([o_near, o_side])
    o_next, o_last = turn(o_own, "y", -1), turn(o_own, "y", -3)

    back, w_across, o_next, o_last = lax.optimization_barrier((back, w_across, o_next, o_last))
    w_corners = [swap(piece, "c") for piece in w_sides]
    w_all = pl.pallas_call(
        join_kernel,
        out_shape=shape((G * Y, bw, 3 * HC), bf16),
        in_specs=[whole()] * 6,
        out_specs=whole(),
        compiler_params=params(),
    )(w_mine, w_across, *w_sides, *w_corners)

    keep, send = pl.pallas_call(
        functools.partial(norm_kernel, fw),
        out_shape=[shape((G, rows, gw), bf16)] * 2,
        in_specs=[scalar()] + [whole()] * 2,
        out_specs=[whole()] * 2,
        compiler_params=params(),
    )(xi[None], back, modulation)

    back, text_kv = lax.optimization_barrier((back, text_kv))
    picked = pl.pallas_call(
        functools.partial(restore_kernel, fw),
        out_shape=shape((parts, rows, width), bf16),
        in_specs=[whole()],
        out_specs=whole(),
        compiler_params=params(),
    )(back)
    text_count = text_kv.shape[1]
    text_pad = -(-text_count // 128) * 128
    text = jnp.pad(text_kv, ((0, 0), (0, text_pad - text_count), (0, Y * HC - inner)))
    text = lax.dynamic_slice_in_dim(text, yi * HC, HC, axis=2)
    text = jnp.concatenate([text[0], text[1]], axis=-1)


    other = swap(send, "xl")
    keep_1, keep_3 = turn(keep, "y", -1), turn(keep, "y", -3)
    other_1, other_3 = across(send, -1), across(send, -3)
    keep_2, other_2 = turn(keep_1, "y", -1), turn(other_3, "y", 1)

    def project(*blocks):
        return pl.pallas_call(
            qkv_kernel,
            in_specs=[scalar()] + [whole()] * 7,
            out_specs=[whole()] * 2,
            out_shape=[shape((Y * rows, HC), bf16), shape((Y * rows, 2 * HC), bf16)],
            scratch_shapes=[pltpu.VMEM((Y * rows, G * gw), bf16)],
            compiler_params=params(24),
        )((xi * 2 + ci)[None], *blocks, w_all, q_gain[None], k_gain[None])

    q_a, kv_a = project(keep, other, keep_1, keep_3)
    o_next_near, o_last_side = o_next[:1], o_last[1:]
    other_1, text, kv_a, o_next_near, o_last_side = lax.optimization_barrier(
        (other_1, text, kv_a, o_next_near, o_last_side)
    )
    q_b, kv_b = project(other_1, other_3, keep_2, other_2)
    o_own, o_next_near, o_last_side, kv_a, kv_b = lax.optimization_barrier(
        (o_own, o_next_near, o_last_side, kv_a, kv_b)
    )
    o_far = [turn(o_next_near, "y", -1), turn(o_last_side, "y", 1)]
    o_crossed = [swap(o_own, "c"), swap(o_next, "c"), None, swap(o_last, "c")]
    kv_c, kv_d = swap(kv_a, "c"), swap(kv_b, "c")
    count = q_a.shape[0]
    attended = pl.pallas_call(
        functools.partial(attention_kernel, text_count),
        grid=(2,),
        in_specs=[scalar()] + [pl.BlockSpec(memory_space=pl.ANY)] * 7,
        out_specs=pl.BlockSpec((2 * Y, rows, HC), lambda i: (0, 0, 0)),
        out_shape=shape((2 * Y, rows, HC), bf16),
        scratch_shapes=[
            pltpu.VMEM((2, count, HC), bf16),
            pltpu.VMEM((4 * count + text_pad, 2 * HC), bf16),
            pltpu.VMEM((NH, 4 * count + text_pad, HD), bf16),
            pltpu.VMEM((NH, 4 * count + text_pad, HD), bf16),
            pltpu.SemaphoreType.DMA((7,)),
        ],
        compiler_params=params(40),
    )(jnp.stack([yi, xi]), q_a, q_b, kv_a, kv_b, kv_c, kv_d, text)

    attended, o_far = lax.optimization_barrier((attended, o_far))
    o_crossed[2] = [swap(piece, "c") for piece in o_far]
    o_pieces = [o_own, o_next, *o_far, o_last, *o_crossed[:2], *o_crossed[2], o_crossed[3]]
    home = lax.all_to_all(attended, ("y", "xl"), 0, 0)
    return pl.pallas_call(
        functools.partial(out_kernel, fo),
        in_specs=[scalar()]
        + [whole()] * 3
        + [pl.BlockSpec(memory_space=pl.ANY)] * len(o_pieces),
        out_specs=whole(),
        out_shape=shape((parts, rows, width), bf16),
        scratch_shapes=[
            pltpu.VMEM((4 * Y, parts * rows, o_near.shape[0]), bf16),
            pltpu.VMEM((4 * Y,) + o_near.shape, bf16),
            pltpu.SemaphoreType.DMA((len(o_pieces),)),
        ],
        compiler_params=params(32),
    )(jnp.stack([yi, xi, ci]), home, picked, gate, *o_pieces)


def solution(mesh):
    fine = Mesh(np.asarray(mesh.devices).reshape(SIZES), AXES)
    placed = (
        P(("xh", "z"), ("y", "xl", "c"), None),
        P(),
        P(),
        P(),
        P(("y", "xl", "c"), None),
        P(("y", "xl", "c"), None),
        P(),
        P(),
        P(),
    )
    return jax.shard_map(
        on_device,
        mesh=fine,
        in_specs=placed,
        out_specs=P(("xh", "z"), ("y", "xl", "c"), None),
        check_vma=False,
    )
```

time: 176 us -> 144 us (0.82)
  waiting for transfers between devices: 71.5 us -> 44.2 us
  Pallas kernels: 36.8 us -> 33.6 us
  local copies, waits for them, and re-layouts: 10.3 us -> 8.02 us
  other arithmetic: 0.23 us -> 2.3 us
    ppermute x15 -> x11, waiting for transfers between devices: 39.9 us -> 18.7 us  [turn(): return lax.ppermute(x, axis, [(i, (i + by) % n) for i in range(n)])]
    all_to_all x1, waiting for transfers between devices: 18 us -> 0.01 us  [on_device(): back = lax.all_to_all(chosen.reshape(GROUPS, parts, RT, gw), GROUP, 0, 0)]
    ppermute x0 -> x4, waiting for transfers between devices: none -> 17.5 us  [the longest x2 16.9 us: beside(): return lax.ppermute(x, ('xh', 'xl'), [(i, (i + by) % n) for i in range(n)])]
    ppermute x15 -> x11, starting transfers between devices: 23.1 us -> 15.2 us  [turn(): return lax.ppermute(x, axis, [(i, (i + by) % n) for i in range(n)])]
    unnamed x25 -> x21, local copies, waits for them, and re-layouts: 8.4 us -> 2.6 us
    ppermute x8 -> x12, waiting for transfers between devices: 5.62 us -> 0.03 us  [swap(): return lax.ppermute(x, axis, [(0, 1), (1, 0)])]
    ppermute x0 -> x4, starting transfers between devices: none -> 5.44 us  [the longest x2 2.76 us: across(): return lax.ppermute(x, ('y', 'xl'), pairs)]
    pallas_call x2 -> x1, Pallas kernels: 3.64 us -> 0.09 us  [placed_in_order(): pl.pallas_call(functools.partial(place_kernel, order), out_shape=jax.Shap...]
  transfers between devices with their start and end apart: 26 -> 30, of which waited for: 11 -> 10; matrix products, arithmetic and copies ran while one was open for 3% -> 6% of each run, Pallas kernels for 17% -> 14%
where the time goes in v2:
time: 144 us; the launch traced here: 143 us
  starting transfers between devices  54 us (38%)
  waiting for transfers between devices  44.2 us (31%)
  Pallas kernels  33.6 us (23%)
  local copies, waits for them, and re-layouts  8.02 us (6%)
  other arithmetic  2.3 us (2%)
    ppermute x11, waiting for transfers between devices, turn(): return lax.ppermute(x, axis, [(i, (i + by) % n) for i in range(n)])  18.7 us
    ppermute x2, waiting for transfers between devices, beside(): return lax.ppermute(x, ('xh', 'xl'), [(i, (i + by) % n) for i in range(n)])  16.9 us
    ppermute x11, starting transfers between devices, turn(): return lax.ppermute(x, axis, [(i, (i + by) % n) for i in range(n)])  15.2 us
    all_to_all x1, starting transfers between devices, on_device(): chunks = lax.all_to_all(packed, GROUP, 0, 0)  11.7 us
    pallas_call x1, Pallas kernels, on_device(): pl.pallas_call(functools.partial(attention_kernel, text_count), grid=(2,)...  10.5 us
    pallas_call x2, Pallas kernels, project(): pl.pallas_call(qkv_kernel, in_specs=[scalar()] + [whole()] * 7, out_specs...  10.5 us
    all_to_all x1, starting transfers between devices, on_device(): back = lax.all_to_all(chosen.reshape(GROUPS, parts, RT, gw), GROUP, 0, 0)  9.65 us
    all_to_all x1, waiting for transfers between devices, on_device(): home = lax.all_to_all(attended, ('y', 'xl'), 0, 0)  7.86 us
  transfers between devices with their start and end apart: 30, of which 10 were waited for; matrix products, arithmetic and copies ran while one was open for 6% of the time, Pallas kernels for 14%

profile of v2, /device:TPU:1, one launch (start us, length us, event | category | flops | bytes accessed | tf_op | source)
XLA Modules:
  0.0 143.2 jit_solution(16034638287668818735)
XLA Ops:
  2.3 11.7 %all-to-all-start = ((bf16[16,2,16,640]{3,2,1,0:T(8,128)(2,1)}), bf16[16,2,16,640]{3,2,1,0:T(8,128)(2,1)S(1)}, u32[]{:S(2)}, u32[]{:S(2)}) async-start(bf16[16,2,16,640]{3,2,1,0:T(8,128)(2,1)} %shard_map.91), calls=%async_computation | async-start | bytes 1310720 | tf_op jit(solution)/shard_map/all_to_all | solution.py:286
  16.4 2.6 %collective-permute-start.1 = (bf16[160,960]{1,0:T(8,128)(2,1)S(1)}, bf16[160,960]{1,0:T(8,128)(2,1)S(1)}, u32[]{:S(2)}, u32[]{:S(2)}) collective-permute-start(bf16[160,960]{1,0:T(8,128)(2,1)S(1)} %get-tuple-element.84), channel_id=1, source_target_pairs={{0,8},{4,12},{8,0},{12,4},{1,9},{5,13},{9,1},{13,5},{2,10},{6,14},... | collective-permute-start | bytes 921608 | tf_op jit(solution)/shard_map/ppermute | solution.py:43
  20.1 4.3 %collective-permute-done.refs_1_ = bf16[160,960]{1,0:T(8,128)(2,1)S(1)} collective-permute-done((bf16[160,960]{1,0:T(8,128)(2,1)S(1)}, bf16[160,960]{1,0:T(8,128)(2,1)S(1)}, u32[]{:S(2)}, u32[]{:S(2)}) %collective-permute-start) | collective-permute-done | bytes 307232 | tf_op jit(solution)/shard_map/ppermute | solution.py:43
  24.4 8.1 %collective-permute-done.1.refs_2_ = bf16[160,960]{1,0:T(8,128)(2,1)S(1)} collective-permute-done((bf16[160,960]{1,0:T(8,128)(2,1)S(1)}, bf16[160,960]{1,0:T(8,128)(2,1)S(1)}, u32[]{:S(2)}, u32[]{:S(2)}) %collective-permute-start.1) | collective-permute-done | bytes 307232 | tf_op jit(solution)/shard_map/ppermute | solution.py:43
  34.3 2.1 %collective-permute-start.4 = (bf16[4,160,960]{2,1,0:T(8,128)(2,1)S(1)}, bf16[4,160,960]{2,1,0:T(8,128)(2,1)}, u32[]{:S(2)}, u32[]{:S(2)}) collective-permute-start(bf16[4,160,960]{2,1,0:T(8,128)(2,1)S(1)} %shard_map.94.refs_0_), channel_id=1, source_target_pairs={{0,1},{1,0},{2,3},{3,2},{4,5},{5,4},{6,7},{7,6},{8,9},{9,8},{10,11... | collective-permute-start | bytes 3686408 | tf_op jit(solution)/shard_map/ppermute | solution.py:38
  36.4 9.7 %all-to-all-start.1 = ((bf16[16,2,16,640]{3,2,1,0:T(8,128)(2,1)}), bf16[16,2,16,640]{3,2,1,0:T(8,128)(2,1)S(1)}, u32[]{:S(2)}, u32[]{:S(2)}) async-start(bf16[16,2,16,640]{3,2,1,0:T(8,128)(2,1)} %bitcast.9), calls=%async_computation.1 | async-start | bytes 1310720 | tf_op jit(solution)/shard_map/all_to_all | solution.py:316
  47.2 2.7 %collective-permute-start.11 = (bf16[2,160,960]{2,1,0:T(8,128)(2,1)}, bf16[2,160,960]{2,1,0:T(8,128)(2,1)}, u32[]{:S(2)}, u32[]{:S(2)}) collective-permute-start(bf16[2,160,960]{2,1,0:T(8,128)(2,1)} %get-tuple-element.81), channel_id=1, source_target_pairs={{0,130},{2,0},{128,2},{130,128},{1,131},{3,1},{129,3},{131,129},{4... | collective-permute-start | bytes 1843208 | tf_op jit(solution)/shard_map/ppermute | solution.py:48
  49.9 2.0 %pad_maximum_fusion.refs_0_ = bf16[2,80,2432]{2,1,0:T(8,128)(2,1)} fusion(bf16[1,80,2432]{2,1,0:T(8,128)(2,1)} %bitcast.11, bf16[1,80,2432]{2,1,0:T(8,128)(2,1)S(1)} %bitcast.37), kind=kLoop, calls=%fused_computation.2 | loop fusion | flops 389120 | bytes 1556480 | tf_op jit(solution)/shard_map/stack | solution.py:319
  51.9 1.9 %collective-permute-start.5 = (bf16[2,80,2432]{2,1,0:T(8,128)(2,1)}, bf16[2,80,2432]{2,1,0:T(8,128)(2,1)}, u32[]{:S(2)}, u32[]{:S(2)}) collective-permute-start(bf16[2,80,2432]{2,1,0:T(8,128)(2,1)} %pad_maximum_fusion.refs_0_), channel_id=1, source_target_pairs={{0,12},{4,0},{8,4},{12,8},{1,13},{5,1},{9,5},{13,9},{2,14},{6,2},{... | collective-permute-start | bytes 2334728 | tf_op jit(solution)/shard_map/ppermute | solution.py:43
  54.4 16.9 %collective-permute-done.10.refs_2_ = bf16[2,160,960]{2,1,0:T(8,128)(2,1)S(1)} collective-permute-done((bf16[2,160,960]{2,1,0:T(8,128)(2,1)}, bf16[2,160,960]{2,1,0:T(8,128)(2,1)S(1)}, u32[]{:S(2)}, u32[]{:S(2)}) %collective-permute-start.10) | collective-permute-done | bytes 614432 | tf_op jit(solution)/shard_map/ppermute | solution.py:48
  75.4 1.7 %collective-permute-start.8 = (bf16[4,64,640]{2,1,0:T(8,128)(2,1)}, bf16[4,64,640]{2,1,0:T(8,128)(2,1)}, u32[]{:S(2)}, u32[]{:S(2)}) collective-permute-start(bf16[4,64,640]{2,1,0:T(8,128)(2,1)} %get-tuple-element.55.refs_0_), channel_id=1, source_target_pairs={{0,12},{4,0},{8,4},{12,8},{1,13},{5,1},{9,5},{13,9},{2,14},{6,2},{... | collective-permute-start | bytes 983048 | tf_op jit(solution)/shard_map/ppermute | solution.py:43
  78.8 2.7 %collective-permute-start.14 = (bf16[4,64,640]{2,1,0:T(8,128)(2,1)}, bf16[4,64,640]{2,1,0:T(8,128)(2,1)}, u32[]{:S(2)}, u32[]{:S(2)}) collective-permute-start(bf16[4,64,640]{2,1,0:T(8,128)(2,1)} %get-tuple-element.56), channel_id=1, source_target_pairs={{0,14},{2,12},{4,2},{6,0},{8,6},{10,4},{12,10},{14,8},{1,15},{3,13... | collective-permute-start | bytes 983048 | tf_op jit(solution)/shard_map/ppermute | solution.py:53
  81.5 2.5 %collective-permute-done.8.refs_2_ = bf16[4,64,640]{2,1,0:T(8,128)(2,1)} collective-permute-done((bf16[4,64,640]{2,1,0:T(8,128)(2,1)}, bf16[4,64,640]{2,1,0:T(8,128)(2,1)}, u32[]{:S(2)}, u32[]{:S(2)}) %collective-permute-start.8) | collective-permute-done | bytes 327712 | tf_op jit(solution)/shard_map/ppermute | solution.py:43
  84.0 3.4 %collective-permute-start.16 = (bf16[4,64,640]{2,1,0:T(8,128)(2,1)}, bf16[4,64,640]{2,1,0:T(8,128)(2,1)}, u32[]{:S(2)}, u32[]{:S(2)}) collective-permute-start(bf16[4,64,640]{2,1,0:T(8,128)(2,1)} %collective-permute-done.8.refs_2_), channel_id=1, source_target_pairs={{0,12},{4,0},{8,4},{12,8},{1,13},{5,1},{9,5},{13,9},{2,14},{6,2},{... | collective-permute-start | bytes 983048 | tf_op jit(solution)/shard_map/ppermute | solution.py:43
  91.7 2.2 %shard_map.96.refs_4_ = bf16[16,160,960]{2,1,0:T(8,128)(2,1)S(1)} custom-call(bf16[4,160,960]{2,1,0:T(8,128)(2,1)S(1)} %shard_map.94.refs_0_, bf16[4,160,960]{2,1,0:T(8,128)(2,1)} %collective-permute-done.4.refs_1_, bf16[2,160,960]{2,1,0:T(8,128)(2,1)S(1)} %collective-permute-done.10.refs_2_, bf16[2,160,960]{2,1,0:T(8,128)(2,1)} %collective-permute-done.11.refs_3_, ...), custom_call_target="tpu_custom_call" | custom-call | tf_op jit(solution)/shard_map/pallas_call | solution.py:324
  94.4 1.7 %collective-permute-done.9.refs_3_ = bf16[4,64,640]{2,1,0:T(8,128)(2,1)} collective-permute-done((bf16[4,64,640]{2,1,0:T(8,128)(2,1)}, bf16[4,64,640]{2,1,0:T(8,128)(2,1)}, u32[]{:S(2)}, u32[]{:S(2)}) %collective-permute-start.9) | collective-permute-done | bytes 327712 | tf_op jit(solution)/shard_map/ppermute | solution.py:43
  96.2 5.3 %shard_map.97 = (bf16[256,320]{1,0:T(8,128)(2,1)S(1)}, bf16[256,640]{1,0:T(8,128)(2,1)S(1)}) custom-call(s32[1]{0:T(128)} %bitcast.3.s_ref, bf16[4,64,640]{2,1,0:T(8,128)(2,1)} %get-tuple-element.55.refs_0_, bf16[4,64,640]{2,1,0:T(8,128)(2,1)} %collective-permute-done.7.refs_1_, bf16[4,64,640]{2,1,0:T(8,128)(2,1)} %collective-permute-done.8.refs_2_, ...), custom_call_target="tpu_custom_call" | custom-call | tf_op jit(solution)/shard_map/pallas_call | solution.py:361
  101.4 1.7 %collective-permute-done.17.refs_3_ = bf16[4,64,640]{2,1,0:T(8,128)(2,1)} collective-permute-done((bf16[4,64,640]{2,1,0:T(8,128)(2,1)}, bf16[4,64,640]{2,1,0:T(8,128)(2,1)}, u32[]{:S(2)}, u32[]{:S(2)}) %collective-permute-start.17) | collective-permute-done | bytes 327712 | tf_op jit(solution)/shard_map/ppermute | solution.py:43
  103.2 5.3 %shard_map.98 = (bf16[256,320]{1,0:T(8,128)(2,1)S(1)}, bf16[256,640]{1,0:T(8,128)(2,1)S(1)}) custom-call(s32[1]{0:T(128)} %bitcast.3.s_ref, bf16[4,64,640]{2,1,0:T(8,128)(2,1)} %collective-permute-done.14.refs_0_, bf16[4,64,640]{2,1,0:T(8,128)(2,1)} %collective-permute-done.15.refs_1_, bf16[4,64,640]{2,1,0:T(8,128)(2,1)} %collective-permute-done.16.refs_2_, ...), custom_call_target="tpu_custom_call" | custom-call | tf_op jit(solution)/shard_map/pallas_call | solution.py:361
  109.1 2.4 %collective-permute-start.20 = (bf16[1,80,2432]{2,1,0:T(8,128)(2,1)S(1)}, bf16[1,80,2432]{2,1,0:T(8,128)(2,1)S(1)}, u32[]{:S(2)}, u32[]{:S(2)}) collective-permute-start(bf16[1,80,2432]{2,1,0:T(8,128)(2,1)S(1)} %slice.44), channel_id=1, source_target_pairs={{0,12},{4,0},{8,4},{12,8},{1,13},{5,1},{9,5},{13,9},{2,14},{6,2},{... | collective-permute-start | bytes 1167368 | tf_op jit(solution)/shard_map/ppermute | solution.py:43
  112.8 10.5 %shard_map.99 = bf16[8,64,320]{2,1,0:T(8,128)(2,1)} custom-call(s32[2]{0:T(128)S(1)} %pad_add_fusion.1.s_ref, bf16[256,320]{1,0:T(8,128)(2,1)S(1)} %get-tuple-element.58.refs_0_, bf16[256,320]{1,0:T(8,128)(2,1)S(1)} %get-tuple-element.64.refs_1_, bf16[256,640]{1,0:T(8,128)(2,1)S(1)} %get-tuple-element.69.refs_2_, ...), custom_call_target="tpu_custom_call" | custom-call | tf_op jit(solution)/shard_map/pallas_call | solution.py:383
  124.3 5.0 %all-to-all-start.2 = ((bf16[8,64,320]{2,1,0:T(8,128)(2,1)}), bf16[8,64,320]{2,1,0:T(8,128)(2,1)S(1)}, u32[]{:S(2)}, u32[]{:S(2)}) async-start(bf16[8,64,320]{2,1,0:T(8,128)(2,1)} %shard_map.99), calls=%async_computation.2 | async-start | bytes 786432 | tf_op jit(solution)/shard_map/all_to_all | solution.py:402
  129.7 7.9 %all-to-all-done.2.h_ref = bf16[8,64,320]{2,1,0:T(8,128)(2,1)S(1)} async-done(((bf16[8,64,320]{2,1,0:T(8,128)(2,1)}), bf16[8,64,320]{2,1,0:T(8,128)(2,1)S(1)}, u32[]{:S(2)}, u32[]{:S(2)}) %all-to-all-start.2) | async-done | bytes 327712 | tf_op jit(solution)/shard_map/all_to_all | solution.py:402
  137.5 5.5 %shard_map.101 = bf16[2,64,2432]{2,1,0:T(8,128)(2,1)} custom-call(s32[3]{0:T(128)S(1)} %pad_add_fusion.s_ref, bf16[8,64,320]{2,1,0:T(8,128)(2,1)S(1)} %all-to-all-done.2.h_ref, bf16[2,64,2432]{2,1,0:T(8,128)(2,1)S(1)} %shard_map.100.x_ref, f32[1,2432]{1,0:T(1,128)S(1)} %dynamic-slice_bitcast_fusion.m_ref, bf16[2,80,2432]{2,1,0:T(8,128)(2,1)} %pad_maximum_fusion.refs_0_, ...), custom_call_target="tpu_custom_call" | custom-call | tf_op jit(solution)/shard_map/pallas_call | solution.py:403
  (82 shorter events, 22.3 us)
Async XLA Ops:
  2.3 30.3 %all-to-all-start = ((bf16[16,2,16,640]{3,2,1,0:T(8,128)(2,1)}), bf16[16,2,16,640]{3,2,1,0:T(8,128)(2,1)S(1)}, u32[]{:S(2)}, u32[]{:S(2)}) async-start(bf16[16,2,16,640]{3,2,1,0:T(8,128)(2,1)} %shard_map.91), calls=%async_computation | async-start | bytes 1310720 | tf_op jit(solution)/shard_map/all_to_all | solution.py:286
  14.1 18.6 %collective-permute-start.3 = (bf16[80,2432]{1,0:T(8,128)(2,1)S(1)}, bf16[80,2432]{1,0:T(8,128)(2,1)}, u32[]{:S(2)}, u32[]{:S(2)}) collective-permute-start(bf16[80,2432]{1,0:T(8,128)(2,1)S(1)} %pad.13), channel_id=1, source_target_pairs={{0,2},{2,0},{1,3},{3,1},{4,6},{6,4},{5,7},{7,5},{8,10},{10,8},{9,1... | collective-permute-start | bytes 1167368 | tf_op jit(solution)/shard_map/ppermute | solution.py:38
  16.4 16.1 %collective-permute-start.1 = (bf16[160,960]{1,0:T(8,128)(2,1)S(1)}, bf16[160,960]{1,0:T(8,128)(2,1)S(1)}, u32[]{:S(2)}, u32[]{:S(2)}) collective-permute-start(bf16[160,960]{1,0:T(8,128)(2,1)S(1)} %get-tuple-element.84), channel_id=1, source_target_pairs={{0,8},{4,12},{8,0},{12,4},{1,9},{5,13},{9,1},{13,5},{2,10},{6,14},... | collective-permute-start | bytes 921608 | tf_op jit(solution)/shard_map/ppermute | solution.py:43
  19.0 13.7 %collective-permute-start.2 = (bf16[160,960]{1,0:T(8,128)(2,1)S(1)}, bf16[160,960]{1,0:T(8,128)(2,1)S(1)}, u32[]{:S(2)}, u32[]{:S(2)}) collective-permute-start(bf16[160,960]{1,0:T(8,128)(2,1)S(1)} %get-tuple-element.83), channel_id=1, source_target_pairs={{0,12},{4,0},{8,4},{12,8},{1,13},{5,1},{9,5},{13,9},{2,14},{6,2},{... | collective-permute-start | bytes 921608 | tf_op jit(solution)/shard_map/ppermute | solution.py:43
  34.3 38.8 %collective-permute-start.4 = (bf16[4,160,960]{2,1,0:T(8,128)(2,1)S(1)}, bf16[4,160,960]{2,1,0:T(8,128)(2,1)}, u32[]{:S(2)}, u32[]{:S(2)}) collective-permute-start(bf16[4,160,960]{2,1,0:T(8,128)(2,1)S(1)} %shard_map.94.refs_0_), channel_id=1, source_target_pairs={{0,1},{1,0},{2,3},{3,2},{4,5},{5,4},{6,7},{7,6},{8,9},{9,8},{10,11... | collective-permute-start | bytes 3686408 | tf_op jit(solution)/shard_map/ppermute | solution.py:38
  36.4 36.6 %all-to-all-start.1 = ((bf16[16,2,16,640]{3,2,1,0:T(8,128)(2,1)}), bf16[16,2,16,640]{3,2,1,0:T(8,128)(2,1)S(1)}, u32[]{:S(2)}, u32[]{:S(2)}) async-start(bf16[16,2,16,640]{3,2,1,0:T(8,128)(2,1)} %bitcast.9), calls=%async_computation.1 | async-start | bytes 1310720 | tf_op jit(solution)/shard_map/all_to_all | solution.py:316
  47.2 24.1 %collective-permute-start.10 = (bf16[2,160,960]{2,1,0:T(8,128)(2,1)}, bf16[2,160,960]{2,1,0:T(8,128)(2,1)S(1)}, u32[]{:S(2)}, u32[]{:S(2)}) collective-permute-start(bf16[2,160,960]{2,1,0:T(8,128)(2,1)} %get-tuple-element.82), channel_id=1, source_target_pairs={{0,2},{2,128},{128,130},{130,0},{1,3},{3,129},{129,131},{131,1},{4... | collective-permute-start | bytes 1843208 | tf_op jit(solution)/shard_map/ppermute | solution.py:48
  47.2 24.9 %collective-permute-start.11 = (bf16[2,160,960]{2,1,0:T(8,128)(2,1)}, bf16[2,160,960]{2,1,0:T(8,128)(2,1)}, u32[]{:S(2)}, u32[]{:S(2)}) collective-permute-start(bf16[2,160,960]{2,1,0:T(8,128)(2,1)} %get-tuple-element.81), channel_id=1, source_target_pairs={{0,130},{2,0},{128,2},{130,128},{1,131},{3,1},{129,3},{131,129},{4... | collective-permute-start | bytes 1843208 | tf_op jit(solution)/shard_map/ppermute | solution.py:48
  51.9 20.9 %collective-permute-start.5 = (bf16[2,80,2432]{2,1,0:T(8,128)(2,1)}, bf16[2,80,2432]{2,1,0:T(8,128)(2,1)}, u32[]{:S(2)}, u32[]{:S(2)}) collective-permute-start(bf16[2,80,2432]{2,1,0:T(8,128)(2,1)} %pad_maximum_fusion.refs_0_), channel_id=1, source_target_pairs={{0,12},{4,0},{8,4},{12,8},{1,13},{5,1},{9,5},{13,9},{2,14},{6,2},{... | collective-permute-start | bytes 2334728 | tf_op jit(solution)/shard_map/ppermute | solution.py:43
  53.8 19.2 %collective-permute-start.6 = (bf16[2,80,2432]{2,1,0:T(8,128)(2,1)}, bf16[2,80,2432]{2,1,0:T(8,128)(2,1)}, u32[]{:S(2)}, u32[]{:S(2)}) collective-permute-start(bf16[2,80,2432]{2,1,0:T(8,128)(2,1)} %pad_maximum_fusion.refs_0_), channel_id=1, source_target_pairs={{0,4},{4,8},{8,12},{12,0},{1,5},{5,9},{9,13},{13,1},{2,6},{6,10},{... | collective-permute-start | bytes 2334728 | tf_op jit(solution)/shard_map/ppermute | solution.py:43
  77.1 10.9 %collective-permute-start.15 = (bf16[4,64,640]{2,1,0:T(8,128)(2,1)}, bf16[4,64,640]{2,1,0:T(8,128)(2,1)}, u32[]{:S(2)}, u32[]{:S(2)}) collective-permute-start(bf16[4,64,640]{2,1,0:T(8,128)(2,1)} %get-tuple-element.56), channel_id=1, source_target_pairs={{0,6},{2,4},{4,10},{6,8},{8,14},{10,12},{12,2},{14,0},{1,7},{3,5},... | collective-permute-start | bytes 983048 | tf_op jit(solution)/shard_map/ppermute | solution.py:53
  77.1 17.3 %collective-permute-start.7 = (bf16[4,64,640]{2,1,0:T(8,128)(2,1)}, bf16[4,64,640]{2,1,0:T(8,128)(2,1)}, u32[]{:S(2)}, u32[]{:S(2)}) collective-permute-start(bf16[4,64,640]{2,1,0:T(8,128)(2,1)} %get-tuple-element.56), channel_id=1, source_target_pairs={{0,2},{2,0},{1,3},{3,1},{4,6},{6,4},{5,7},{7,5},{8,10},{10,8},{9,1... | collective-permute-start | bytes 983048 | tf_op jit(solution)/shard_map/ppermute | solution.py:38
  78.0 18.1 %collective-permute-start.9 = (bf16[4,64,640]{2,1,0:T(8,128)(2,1)}, bf16[4,64,640]{2,1,0:T(8,128)(2,1)}, u32[]{:S(2)}, u32[]{:S(2)}) collective-permute-start(bf16[4,64,640]{2,1,0:T(8,128)(2,1)} %get-tuple-element.55.refs_0_), channel_id=1, source_target_pairs={{0,4},{4,8},{8,12},{12,0},{1,5},{5,9},{9,13},{13,1},{2,6},{6,10},{... | collective-permute-start | bytes 983048 | tf_op jit(solution)/shard_map/ppermute | solution.py:43
  78.8 22.6 %collective-permute-start.14 = (bf16[4,64,640]{2,1,0:T(8,128)(2,1)}, bf16[4,64,640]{2,1,0:T(8,128)(2,1)}, u32[]{:S(2)}, u32[]{:S(2)}) collective-permute-start(bf16[4,64,640]{2,1,0:T(8,128)(2,1)} %get-tuple-element.56), channel_id=1, source_target_pairs={{0,14},{2,12},{4,2},{6,0},{8,6},{10,4},{12,10},{14,8},{1,15},{3,13... | collective-permute-start | bytes 983048 | tf_op jit(solution)/shard_map/ppermute | solution.py:53
  84.0 17.4 %collective-permute-start.16 = (bf16[4,64,640]{2,1,0:T(8,128)(2,1)}, bf16[4,64,640]{2,1,0:T(8,128)(2,1)}, u32[]{:S(2)}, u32[]{:S(2)}) collective-permute-start(bf16[4,64,640]{2,1,0:T(8,128)(2,1)} %collective-permute-done.8.refs_2_), channel_id=1, source_target_pairs={{0,12},{4,0},{8,4},{12,8},{1,13},{5,1},{9,5},{13,9},{2,14},{6,2},{... | collective-permute-start | bytes 983048 | tf_op jit(solution)/shard_map/ppermute | solution.py:43
  88.0 15.2 %collective-permute-start.17 = (bf16[4,64,640]{2,1,0:T(8,128)(2,1)}, bf16[4,64,640]{2,1,0:T(8,128)(2,1)}, u32[]{:S(2)}, u32[]{:S(2)}) collective-permute-start(bf16[4,64,640]{2,1,0:T(8,128)(2,1)} %collective-permute-done.15.refs_1_), channel_id=1, source_target_pairs={{0,4},{4,8},{8,12},{12,0},{1,5},{5,9},{9,13},{13,1},{2,6},{6,10},{... | collective-permute-start | bytes 983048 | tf_op jit(solution)/shard_map/ppermute | solution.py:43
  109.1 14.2 %collective-permute-start.20 = (bf16[1,80,2432]{2,1,0:T(8,128)(2,1)S(1)}, bf16[1,80,2432]{2,1,0:T(8,128)(2,1)S(1)}, u32[]{:S(2)}, u32[]{:S(2)}) collective-permute-start(bf16[1,80,2432]{2,1,0:T(8,128)(2,1)S(1)} %slice.44), channel_id=1, source_target_pairs={{0,12},{4,0},{8,4},{12,8},{1,13},{5,1},{9,5},{13,9},{2,14},{6,2},{... | collective-permute-start | bytes 1167368 | tf_op jit(solution)/shard_map/ppermute | solution.py:43
  111.5 11.8 %collective-permute-start.21 = (bf16[1,80,2432]{2,1,0:T(8,128)(2,1)S(1)}, bf16[1,80,2432]{2,1,0:T(8,128)(2,1)}, u32[]{:S(2)}, u32[]{:S(2)}) collective-permute-start(bf16[1,80,2432]{2,1,0:T(8,128)(2,1)S(1)} %slice.45), channel_id=1, source_target_pairs={{0,4},{4,8},{8,12},{12,0},{1,5},{5,9},{9,13},{13,1},{2,6},{6,10},{... | collective-permute-start | bytes 1167368 | tf_op jit(solution)/shard_map/ppermute | solution.py:43
  111.5 18.1 %collective-permute-start.23 = (bf16[2,80,2432]{2,1,0:T(8,128)(2,1)}, bf16[2,80,2432]{2,1,0:T(8,128)(2,1)}, u32[]{:S(2)}, u32[]{:S(2)}) collective-permute-start(bf16[2,80,2432]{2,1,0:T(8,128)(2,1)} %collective-permute-done.5.refs_1_), channel_id=1, source_target_pairs={{0,1},{1,0},{2,3},{3,2},{4,5},{5,4},{6,7},{7,6},{8,9},{9,8},{10,11... | collective-permute-start | bytes 2334728 | tf_op jit(solution)/shard_map/ppermute | solution.py:38
  112.2 17.5 %collective-permute-start.26 = (bf16[2,80,2432]{2,1,0:T(8,128)(2,1)}, bf16[2,80,2432]{2,1,0:T(8,128)(2,1)}, u32[]{:S(2)}, u32[]{:S(2)}) collective-permute-start(bf16[2,80,2432]{2,1,0:T(8,128)(2,1)} %collective-permute-done.6.refs_4_), channel_id=1, source_target_pairs={{0,1},{1,0},{2,3},{3,2},{4,5},{5,4},{6,7},{7,6},{8,9},{9,8},{10,11... | collective-permute-start | bytes 2334728 | tf_op jit(solution)/shard_map/ppermute | solution.py:38
  112.5 25.0 %collective-permute-start.22 = (bf16[2,80,2432]{2,1,0:T(8,128)(2,1)}, bf16[2,80,2432]{2,1,0:T(8,128)(2,1)}, u32[]{:S(2)}, u32[]{:S(2)}) collective-permute-start(bf16[2,80,2432]{2,1,0:T(8,128)(2,1)} %pad_maximum_fusion.refs_0_), channel_id=1, source_target_pairs={{0,1},{1,0},{2,3},{3,2},{4,5},{5,4},{6,7},{7,6},{8,9},{9,8},{10,11... | collective-permute-start | bytes 2334728 | tf_op jit(solution)/shard_map/ppermute | solution.py:38
  123.4 14.2 %collective-permute-start.24 = (bf16[1,80,2432]{2,1,0:T(8,128)(2,1)S(1)}, bf16[1,80,2432]{2,1,0:T(8,128)(2,1)}, u32[]{:S(2)}, u32[]{:S(2)}) collective-permute-start(bf16[1,80,2432]{2,1,0:T(8,128)(2,1)S(1)} %collective-permute-done.20.refs_2_), channel_id=1, source_target_pairs={{0,1},{1,0},{2,3},{3,2},{4,5},{5,4},{6,7},{7,6},{8,9},{9,8},{10,11... | collective-permute-start | bytes 1167368 | tf_op jit(solution)/shard_map/ppermute | solution.py:38
  124.3 13.3 %collective-permute-start.25 = (bf16[1,80,2432]{2,1,0:T(8,128)(2,1)}, bf16[1,80,2432]{2,1,0:T(8,128)(2,1)}, u32[]{:S(2)}, u32[]{:S(2)}) collective-permute-start(bf16[1,80,2432]{2,1,0:T(8,128)(2,1)} %collective-permute-done.21.refs_3_), channel_id=1, source_target_pairs={{0,1},{1,0},{2,3},{3,2},{4,5},{5,4},{6,7},{7,6},{8,9},{9,8},{10,11... | collective-permute-start | bytes 1167368 | tf_op jit(solution)/shard_map/ppermute | solution.py:38
  124.3 13.2 %all-to-all-start.2 = ((bf16[8,64,320]{2,1,0:T(8,128)(2,1)}), bf16[8,64,320]{2,1,0:T(8,128)(2,1)S(1)}, u32[]{:S(2)}, u32[]{:S(2)}) async-start(bf16[8,64,320]{2,1,0:T(8,128)(2,1)} %shard_map.99), calls=%async_computation.2 | async-start | bytes 786432 | tf_op jit(solution)/shard_map/all_to_all | solution.py:402
  (16 other events, 164.7 us)

commit v3 on v2

--- a/solution.py
+++ b/solution.py
@@ -298,7 +298,13 @@
     o_near = jnp.pad(w_out, ((0, -fo % RT), (0, 0)))
     o_side = swap(o_near, "xl")
 
-    chunks, w_pieces, o_side = lax.optimization_barrier((chunks, w_pieces, o_side))
+    text_count = text_kv.shape[1]
+    text_pad = -(-text_count // 128) * 128
+    text = jnp.pad(text_kv, ((0, 0), (0, text_pad - text_count), (0, Y * HC - inner)))
+    text = lax.dynamic_slice_in_dim(text, yi * HC, HC, axis=2)
+    text = jnp.concatenate([text[0], text[1]], axis=-1)
+
+    chunks, w_pieces, o_side, text = lax.optimization_barrier((chunks, w_pieces, o_side, text))
     w_mine = placed_in_order(lambda k, s: (s[0] - k) & 3, yi[None], w_pieces)
 
     modulation = lax.dynamic_index_in_dim(mod_table, timestep[0], 0, keepdims=False)
@@ -337,7 +343,6 @@
         compiler_params=params(),
     )(xi[None], back, modulation)
 
-    back, text_kv = lax.optimization_barrier((back, text_kv))
     picked = pl.pallas_call(
         functools.partial(restore_kernel, fw),
         out_shape=shape((parts, rows, width), bf16),
@@ -345,13 +350,6 @@
         out_specs=whole(),
         compiler_params=params(),
     )(back)
-    text_count = text_kv.shape[1]
-    text_pad = -(-text_count // 128) * 128
-    text = jnp.pad(text_kv, ((0, 0), (0, text_pad - text_count), (0, Y * HC - inner)))
-    text = lax.dynamic_slice_in_dim(text, yi * HC, HC, axis=2)
-    text = jnp.concatenate([text[0], text[1]], axis=-1)
-
-
     other = swap(send, "xl")
     keep_1, keep_3 = turn(keep, "y", -1), turn(keep, "y", -3)
     other_1, other_3 = across(send, -1), across(send, -3)
@@ -369,8 +367,8 @@
 
     q_a, kv_a = project(keep, other, keep_1, keep_3)
     o_next_near, o_last_side = o_next[:1], o_last[1:]
-    other_1, text, kv_a, o_next_near, o_last_side = lax.optimization_barrier(
-        (other_1, text, kv_a, o_next_near, o_last_side)
+    other_1, kv_a, o_next_near, o_last_side = lax.optimization_barrier(
+        (other_1, kv_a, o_next_near, o_last_side)
     )
     q_b, kv_b = project(other_1, other_3, keep_2, other_2)
     o_own, o_next_near, o_last_side, kv_a, kv_b = lax.optimization_barrier(

time: 144 us -> 144 us (level)
  local copies, waits for them, and re-layouts: 8.02 us -> 12 us
  waiting for transfers between devices: 44.2 us -> 41.7 us
    unnamed x21 -> x24, local copies, waits for them, and re-layouts: 2.6 us -> 5.49 us
    ppermute x11, waiting for transfers between devices: 18.7 us -> 15.9 us  [turn(): return lax.ppermute(x, axis, [(i, (i + by) % n) for i in range(n)])]
    ppermute x11, starting transfers between devices: 15.2 us -> 12.8 us  [turn(): return lax.ppermute(x, axis, [(i, (i + by) % n) for i in range(n)])]
    optimization_barrier x1 -> x0, local copies, waits for them, and re-layouts: 1.62 us -> none  [on_device(): back, text_kv = lax.optimization_barrier((back, text_kv))]
  transfers between devices with their start and end apart: 30 -> 30, of which waited for: 10 -> 8; matrix products, arithmetic and copies ran while one was open for 6% -> 8% of each run, Pallas kernels for 14% -> 14%
where the time goes in v3:
time: 144 us
  starting transfers between devices  53 us (37%)
  waiting for transfers between devices  41.7 us (29%)
  Pallas kernels  33.6 us (23%)
  local copies, waits for them, and re-layouts  12 us (8%)
  other arithmetic  2.4 us (2%)
    ppermute x2, waiting for transfers between devices, beside(): return lax.ppermute(x, ('xh', 'xl'), [(i, (i + by) % n) for i in range(n)])  17.2 us
    ppermute x11, waiting for transfers between devices, turn(): return lax.ppermute(x, axis, [(i, (i + by) % n) for i in range(n)])  15.9 us
    ppermute x11, starting transfers between devices, turn(): return lax.ppermute(x, axis, [(i, (i + by) % n) for i in range(n)])  12.8 us
    all_to_all x1, starting transfers between devices, on_device(): chunks = lax.all_to_all(packed, GROUP, 0, 0)  11.7 us
    pallas_call x1, Pallas kernels, on_device(): pl.pallas_call(functools.partial(attention_kernel, text_count), grid=(2,)...  10.5 us
    pallas_call x2, Pallas kernels, project(): pl.pallas_call(qkv_kernel, in_specs=[scalar()] + [whole()] * 7, out_specs...  10.5 us
    all_to_all x1, starting transfers between devices, on_device(): back = lax.all_to_all(chosen.reshape(GROUPS, parts, RT, gw), GROUP, 0, 0)  9.66 us
    all_to_all x1, waiting for transfers between devices, on_device(): home = lax.all_to_all(attended, ('y', 'xl'), 0, 0)  7.86 us
  transfers between devices with their start and end apart: 30, of which 8 were waited for; matrix products, arithmetic and copies ran while one was open for 8% of the time, Pallas kernels for 14%

profile of v3, /device:TPU:1, one launch (start us, length us, event | category | flops | bytes accessed | tf_op | source)
XLA Modules:
  0.0 143.8 jit_solution(1304418469143708737)
XLA Ops:
  2.3 11.7 %all-to-all-start = ((bf16[16,2,16,640]{3,2,1,0:T(8,128)(2,1)}), bf16[16,2,16,640]{3,2,1,0:T(8,128)(2,1)S(1)}, u32[]{:S(2)}, u32[]{:S(2)}) async-start(bf16[16,2,16,640]{3,2,1,0:T(8,128)(2,1)} %shard_map.91), calls=%async_computation | async-start | bytes 1310720 | tf_op jit(solution)/shard_map/all_to_all | solution.py:286
  17.8 2.6 %collective-permute-start.1 = (bf16[160,960]{1,0:T(8,128)(2,1)}, bf16[160,960]{1,0:T(8,128)(2,1)S(1)}, u32[]{:S(2)}, u32[]{:S(2)}) collective-permute-start(bf16[160,960]{1,0:T(8,128)(2,1)} %get-tuple-element.80), channel_id=1, source_target_pairs={{0,8},{4,12},{8,0},{12,4},{1,9},{5,13},{9,1},{13,5},{2,10},{6,14},... | collective-permute-start | bytes 921608 | tf_op jit(solution)/shard_map/ppermute | solution.py:43
  21.5 2.8 %copy.11 = bf16[2,333,1216]{2,1,0:T(8,128)(2,1)} copy(bf16[2,333,1216]{2,0,1:T(2,128)(2,1)} %param.17) | data formatting | bytes 3239424 | tf_op args[8]
  26.0 8.1 %collective-permute-done.1.refs_2_ = bf16[160,960]{1,0:T(8,128)(2,1)S(1)} collective-permute-done((bf16[160,960]{1,0:T(8,128)(2,1)}, bf16[160,960]{1,0:T(8,128)(2,1)S(1)}, u32[]{:S(2)}, u32[]{:S(2)}) %collective-permute-start.1) | collective-permute-done | bytes 307232 | tf_op jit(solution)/shard_map/ppermute | solution.py:43
  35.6 1.5 %shard_map.93 = bf16[32,16,640]{2,1,0:T(8,128)(2,1)} custom-call(s32[32]{0:T(128)S(1)} %copy-done.8, bf16[32,16,640]{2,1,0:T(8,128)(2,1)S(1)} %bitcast.31), custom_call_target="tpu_custom_call" | custom-call | tf_op jit(solution)/shard_map/pallas_call | solution.py:313
  37.2 2.2 %collective-permute-start.4 = (bf16[4,160,960]{2,1,0:T(8,128)(2,1)S(1)}, bf16[4,160,960]{2,1,0:T(8,128)(2,1)}, u32[]{:S(2)}, u32[]{:S(2)}) collective-permute-start(bf16[4,160,960]{2,1,0:T(8,128)(2,1)S(1)} %shard_map.94.refs_0_), channel_id=1, source_target_pairs={{0,1},{1,0},{2,3},{3,2},{4,5},{5,4},{6,7},{7,6},{8,9},{9,8},{10,11... | collective-permute-start | bytes 3686408 | tf_op jit(solution)/shard_map/ppermute | solution.py:38
  39.4 9.7 %all-to-all-start.1 = ((bf16[16,2,16,640]{3,2,1,0:T(8,128)(2,1)}), bf16[16,2,16,640]{3,2,1,0:T(8,128)(2,1)S(1)}, u32[]{:S(2)}, u32[]{:S(2)}) async-start(bf16[16,2,16,640]{3,2,1,0:T(8,128)(2,1)} %bitcast.11), calls=%async_computation.1 | async-start | bytes 1310720 | tf_op jit(solution)/shard_map/all_to_all | solution.py:322
  50.3 2.7 %collective-permute-start.11 = (bf16[2,160,960]{2,1,0:T(8,128)(2,1)}, bf16[2,160,960]{2,1,0:T(8,128)(2,1)}, u32[]{:S(2)}, u32[]{:S(2)}) collective-permute-start(bf16[2,160,960]{2,1,0:T(8,128)(2,1)} %get-tuple-element.77), channel_id=1, source_target_pairs={{0,130},{2,0},{128,2},{130,128},{1,131},{3,1},{129,3},{131,129},{4... | collective-permute-start | bytes 1843208 | tf_op jit(solution)/shard_map/ppermute | solution.py:48
  53.0 2.1 %pad_maximum_fusion.refs_0_ = bf16[2,80,2432]{2,1,0:T(8,128)(2,1)} fusion(bf16[1,80,2432]{2,1,0:T(8,128)(2,1)} %bitcast.13, bf16[1,80,2432]{2,1,0:T(8,128)(2,1)} %bitcast.12), kind=kLoop, calls=%fused_computation.2 | loop fusion | flops 389120 | bytes 1556480 | tf_op jit(solution)/shard_map/stack | solution.py:325
  57.2 17.2 %collective-permute-done.10.refs_2_ = bf16[2,160,960]{2,1,0:T(8,128)(2,1)} collective-permute-done((bf16[2,160,960]{2,1,0:T(8,128)(2,1)}, bf16[2,160,960]{2,1,0:T(8,128)(2,1)}, u32[]{:S(2)}, u32[]{:S(2)}) %collective-permute-start.10) | collective-permute-done | bytes 614432 | tf_op jit(solution)/shard_map/ppermute | solution.py:48
  75.4 1.6 %shard_map.95 = (bf16[4,64,640]{2,1,0:T(8,128)(2,1)}, bf16[4,64,640]{2,1,0:T(8,128)(2,1)}) custom-call(s32[1]{0:T(128)} %bitcast.1.s_ref, bf16[16,2,16,640]{3,2,1,0:T(8,128)(2,1)S(1)} %all-to-all-done.1.x_ref, f32[3,2432]{1,0:T(4,128)S(1)} %bitcast.32), custom_call_target="tpu_custom_call" | custom-call | tf_op jit(solution)/shard_map/pallas_call | solution.py:338
  79.8 2.9 %collective-permute-start.14 = (bf16[4,64,640]{2,1,0:T(8,128)(2,1)}, bf16[4,64,640]{2,1,0:T(8,128)(2,1)}, u32[]{:S(2)}, u32[]{:S(2)}) collective-permute-start(bf16[4,64,640]{2,1,0:T(8,128)(2,1)} %get-tuple-element.54), channel_id=1, source_target_pairs={{0,14},{2,12},{4,2},{6,0},{8,6},{10,4},{12,10},{14,8},{1,15},{3,13... | collective-permute-start | bytes 983048 | tf_op jit(solution)/shard_map/ppermute | solution.py:53
  82.7 1.7 %collective-permute-done.8.refs_2_ = bf16[4,64,640]{2,1,0:T(8,128)(2,1)} collective-permute-done((bf16[4,64,640]{2,1,0:T(8,128)(2,1)}, bf16[4,64,640]{2,1,0:T(8,128)(2,1)}, u32[]{:S(2)}, u32[]{:S(2)}) %collective-permute-start.8) | collective-permute-done | bytes 327712 | tf_op jit(solution)/shard_map/ppermute | solution.py:43
  84.5 3.3 %collective-permute-start.16 = (bf16[4,64,640]{2,1,0:T(8,128)(2,1)}, bf16[4,64,640]{2,1,0:T(8,128)(2,1)}, u32[]{:S(2)}, u32[]{:S(2)}) collective-permute-start(bf16[4,64,640]{2,1,0:T(8,128)(2,1)} %collective-permute-done.8.refs_2_), channel_id=1, source_target_pairs={{0,12},{4,0},{8,4},{12,8},{1,13},{5,1},{9,5},{13,9},{2,14},{6,2},{... | collective-permute-start | bytes 983048 | tf_op jit(solution)/shard_map/ppermute | solution.py:43
  90.6 2.4 %shard_map.96.refs_4_ = bf16[16,160,960]{2,1,0:T(8,128)(2,1)S(1)} custom-call(bf16[4,160,960]{2,1,0:T(8,128)(2,1)S(1)} %shard_map.94.refs_0_, bf16[4,160,960]{2,1,0:T(8,128)(2,1)} %collective-permute-done.4.refs_1_, bf16[2,160,960]{2,1,0:T(8,128)(2,1)} %collective-permute-done.10.refs_2_, bf16[2,160,960]{2,1,0:T(8,128)(2,1)} %collective-permute-done.11.refs_3_, ...), custom_call_target="tpu_custom_call" | custom-call | tf_op jit(solution)/shard_map/pallas_call | solution.py:330
  93.0 4.1 %collective-permute-done.9.refs_3_ = bf16[4,64,640]{2,1,0:T(8,128)(2,1)} collective-permute-done((bf16[4,64,640]{2,1,0:T(8,128)(2,1)}, bf16[4,64,640]{2,1,0:T(8,128)(2,1)}, u32[]{:S(2)}, u32[]{:S(2)}) %collective-permute-start.9) | collective-permute-done | bytes 327712 | tf_op jit(solution)/shard_map/ppermute | solution.py:43
  97.2 5.3 %shard_map.97 = (bf16[256,320]{1,0:T(8,128)(2,1)S(1)}, bf16[256,640]{1,0:T(8,128)(2,1)S(1)}) custom-call(s32[1]{0:T(128)} %bitcast.3.s_ref, bf16[4,64,640]{2,1,0:T(8,128)(2,1)} %get-tuple-element.53.refs_0_, bf16[4,64,640]{2,1,0:T(8,128)(2,1)} %collective-permute-done.7.refs_1_, bf16[4,64,640]{2,1,0:T(8,128)(2,1)} %collective-permute-done.8.refs_2_, ...), custom_call_target="tpu_custom_call" | custom-call | tf_op jit(solution)/shard_map/pallas_call | solution.py:359
  102.4 1.7 %collective-permute-done.17.refs_3_ = bf16[4,64,640]{2,1,0:T(8,128)(2,1)} collective-permute-done((bf16[4,64,640]{2,1,0:T(8,128)(2,1)}, bf16[4,64,640]{2,1,0:T(8,128)(2,1)}, u32[]{:S(2)}, u32[]{:S(2)}) %collective-permute-start.17) | collective-permute-done | bytes 327712 | tf_op jit(solution)/shard_map/ppermute | solution.py:43
  104.2 5.3 %shard_map.98 = (bf16[256,320]{1,0:T(8,128)(2,1)S(1)}, bf16[256,640]{1,0:T(8,128)(2,1)S(1)}) custom-call(s32[1]{0:T(128)} %bitcast.3.s_ref, bf16[4,64,640]{2,1,0:T(8,128)(2,1)} %collective-permute-done.14.refs_0_, bf16[4,64,640]{2,1,0:T(8,128)(2,1)} %collective-permute-done.15.refs_1_, bf16[4,64,640]{2,1,0:T(8,128)(2,1)} %collective-permute-done.16.refs_2_, ...), custom_call_target="tpu_custom_call" | custom-call | tf_op jit(solution)/shard_map/pallas_call | solution.py:359
  110.1 1.8 %collective-permute-start.20 = (bf16[1,80,2432]{2,1,0:T(8,128)(2,1)S(1)}, bf16[1,80,2432]{2,1,0:T(8,128)(2,1)}, u32[]{:S(2)}, u32[]{:S(2)}) collective-permute-start(bf16[1,80,2432]{2,1,0:T(8,128)(2,1)S(1)} %slice.44), channel_id=1, source_target_pairs={{0,12},{4,0},{8,4},{12,8},{1,13},{5,1},{9,5},{13,9},{2,14},{6,2},{... | collective-permute-start | bytes 1167368 | tf_op jit(solution)/shard_map/ppermute | solution.py:43
  113.2 10.5 %shard_map.99 = bf16[8,64,320]{2,1,0:T(8,128)(2,1)} custom-call(s32[2]{0:T(128)S(1)} %pad_add_fusion.1.s_ref, bf16[256,320]{1,0:T(8,128)(2,1)S(1)} %get-tuple-element.56.refs_0_, bf16[256,320]{1,0:T(8,128)(2,1)S(1)} %get-tuple-element.61.refs_1_, bf16[256,640]{1,0:T(8,128)(2,1)S(1)} %get-tuple-element.66.refs_2_, ...), custom_call_target="tpu_custom_call" | custom-call | tf_op jit(solution)/shard_map/pallas_call | solution.py:381
  124.8 5.3 %all-to-all-start.2 = ((bf16[8,64,320]{2,1,0:T(8,128)(2,1)}), bf16[8,64,320]{2,1,0:T(8,128)(2,1)S(1)}, u32[]{:S(2)}, u32[]{:S(2)}) async-start(bf16[8,64,320]{2,1,0:T(8,128)(2,1)} %shard_map.99), calls=%async_computation.2 | async-start | bytes 786432 | tf_op jit(solution)/shard_map/all_to_all | solution.py:400
  130.4 7.9 %all-to-all-done.2.h_ref = bf16[8,64,320]{2,1,0:T(8,128)(2,1)S(1)} async-done(((bf16[8,64,320]{2,1,0:T(8,128)(2,1)}), bf16[8,64,320]{2,1,0:T(8,128)(2,1)S(1)}, u32[]{:S(2)}, u32[]{:S(2)}) %all-to-all-start.2) | async-done | bytes 327712 | tf_op jit(solution)/shard_map/all_to_all | solution.py:400
  138.3 5.3 %shard_map.101 = bf16[2,64,2432]{2,1,0:T(8,128)(2,1)} custom-call(s32[3]{0:T(128)S(1)} %pad_add_fusion.s_ref, bf16[8,64,320]{2,1,0:T(8,128)(2,1)S(1)} %all-to-all-done.2.h_ref, bf16[2,64,2432]{2,1,0:T(8,128)(2,1)S(1)} %shard_map.100.x_ref, f32[1,2432]{1,0:T(1,128)S(1)} %dynamic-slice_bitcast_fusion.m_ref, bf16[2,80,2432]{2,1,0:T(8,128)(2,1)} %pad_maximum_fusion.refs_0_, ...), custom_call_target="tpu_custom_call" | custom-call | tf_op jit(solution)/shard_map/pallas_call | solution.py:401
  (84 shorter events, 22.8 us)
Async XLA Ops:
  2.3 33.3 %all-to-all-start = ((bf16[16,2,16,640]{3,2,1,0:T(8,128)(2,1)}), bf16[16,2,16,640]{3,2,1,0:T(8,128)(2,1)S(1)}, u32[]{:S(2)}, u32[]{:S(2)}) async-start(bf16[16,2,16,640]{3,2,1,0:T(8,128)(2,1)} %shard_map.91), calls=%async_computation | async-start | bytes 1310720 | tf_op jit(solution)/shard_map/all_to_all | solution.py:286
  14.8 20.7 %collective-permute-start.3 = (bf16[80,2432]{1,0:T(8,128)(2,1)}, bf16[80,2432]{1,0:T(8,128)(2,1)}, u32[]{:S(2)}, u32[]{:S(2)}) collective-permute-start(bf16[80,2432]{1,0:T(8,128)(2,1)} %pad.13), channel_id=1, source_target_pairs={{0,2},{2,0},{1,3},{3,1},{4,6},{6,4},{5,7},{7,5},{8,10},{10,8},{9,1... | collective-permute-start | bytes 1167368 | tf_op jit(solution)/shard_map/ppermute | solution.py:38
  17.8 16.4 %collective-permute-start.1 = (bf16[160,960]{1,0:T(8,128)(2,1)}, bf16[160,960]{1,0:T(8,128)(2,1)S(1)}, u32[]{:S(2)}, u32[]{:S(2)}) collective-permute-start(bf16[160,960]{1,0:T(8,128)(2,1)} %get-tuple-element.80), channel_id=1, source_target_pairs={{0,8},{4,12},{8,0},{12,4},{1,9},{5,13},{9,1},{13,5},{2,10},{6,14},... | collective-permute-start | bytes 921608 | tf_op jit(solution)/shard_map/ppermute | solution.py:43
  20.4 14.5 %collective-permute-start.2 = (bf16[160,960]{1,0:T(8,128)(2,1)}, bf16[160,960]{1,0:T(8,128)(2,1)S(1)}, u32[]{:S(2)}, u32[]{:S(2)}) collective-permute-start(bf16[160,960]{1,0:T(8,128)(2,1)} %get-tuple-element.79), channel_id=1, source_target_pairs={{0,12},{4,0},{8,4},{12,8},{1,13},{5,1},{9,5},{13,9},{2,14},{6,2},{... | collective-permute-start | bytes 921608 | tf_op jit(solution)/shard_map/ppermute | solution.py:43
  37.2 38.2 %collective-permute-start.4 = (bf16[4,160,960]{2,1,0:T(8,128)(2,1)S(1)}, bf16[4,160,960]{2,1,0:T(8,128)(2,1)}, u32[]{:S(2)}, u32[]{:S(2)}) collective-permute-start(bf16[4,160,960]{2,1,0:T(8,128)(2,1)S(1)} %shard_map.94.refs_0_), channel_id=1, source_target_pairs={{0,1},{1,0},{2,3},{3,2},{4,5},{5,4},{6,7},{7,6},{8,9},{9,8},{10,11... | collective-permute-start | bytes 3686408 | tf_op jit(solution)/shard_map/ppermute | solution.py:38
  39.4 36.0 %all-to-all-start.1 = ((bf16[16,2,16,640]{3,2,1,0:T(8,128)(2,1)}), bf16[16,2,16,640]{3,2,1,0:T(8,128)(2,1)S(1)}, u32[]{:S(2)}, u32[]{:S(2)}) async-start(bf16[16,2,16,640]{3,2,1,0:T(8,128)(2,1)} %bitcast.11), calls=%async_computation.1 | async-start | bytes 1310720 | tf_op jit(solution)/shard_map/all_to_all | solution.py:322
  50.3 24.1 %collective-permute-start.10 = (bf16[2,160,960]{2,1,0:T(8,128)(2,1)}, bf16[2,160,960]{2,1,0:T(8,128)(2,1)}, u32[]{:S(2)}, u32[]{:S(2)}) collective-permute-start(bf16[2,160,960]{2,1,0:T(8,128)(2,1)} %get-tuple-element.78), channel_id=1, source_target_pairs={{0,2},{2,128},{128,130},{130,0},{1,3},{3,129},{129,131},{131,1},{4... | collective-permute-start | bytes 1843208 | tf_op jit(solution)/shard_map/ppermute | solution.py:48
  50.3 25.0 %collective-permute-start.11 = (bf16[2,160,960]{2,1,0:T(8,128)(2,1)}, bf16[2,160,960]{2,1,0:T(8,128)(2,1)}, u32[]{:S(2)}, u32[]{:S(2)}) collective-permute-start(bf16[2,160,960]{2,1,0:T(8,128)(2,1)} %get-tuple-element.77), channel_id=1, source_target_pairs={{0,130},{2,0},{128,2},{130,128},{1,131},{3,1},{129,3},{131,129},{4... | collective-permute-start | bytes 1843208 | tf_op jit(solution)/shard_map/ppermute | solution.py:48
  55.1 20.3 %collective-permute-start.5 = (bf16[2,80,2432]{2,1,0:T(8,128)(2,1)}, bf16[2,80,2432]{2,1,0:T(8,128)(2,1)}, u32[]{:S(2)}, u32[]{:S(2)}) collective-permute-start(bf16[2,80,2432]{2,1,0:T(8,128)(2,1)} %pad_maximum_fusion.refs_0_), channel_id=1, source_target_pairs={{0,12},{4,0},{8,4},{12,8},{1,13},{5,1},{9,5},{13,9},{2,14},{6,2},{... | collective-permute-start | bytes 2334728 | tf_op jit(solution)/shard_map/ppermute | solution.py:43
  56.2 19.3 %collective-permute-start.6 = (bf16[2,80,2432]{2,1,0:T(8,128)(2,1)}, bf16[2,80,2432]{2,1,0:T(8,128)(2,1)}, u32[]{:S(2)}, u32[]{:S(2)}) collective-permute-start(bf16[2,80,2432]{2,1,0:T(8,128)(2,1)} %pad_maximum_fusion.refs_0_), channel_id=1, source_target_pairs={{0,4},{4,8},{8,12},{12,0},{1,5},{5,9},{9,13},{13,1},{2,6},{6,10},{... | collective-permute-start | bytes 2334728 | tf_op jit(solution)/shard_map/ppermute | solution.py:43
  78.1 10.4 %collective-permute-start.15 = (bf16[4,64,640]{2,1,0:T(8,128)(2,1)}, bf16[4,64,640]{2,1,0:T(8,128)(2,1)}, u32[]{:S(2)}, u32[]{:S(2)}) collective-permute-start(bf16[4,64,640]{2,1,0:T(8,128)(2,1)} %get-tuple-element.54), channel_id=1, source_target_pairs={{0,6},{2,4},{4,10},{6,8},{8,14},{10,12},{12,2},{14,0},{1,7},{3,5},... | collective-permute-start | bytes 983048 | tf_op jit(solution)/shard_map/ppermute | solution.py:53
  78.9 14.1 %collective-permute-start.7 = (bf16[4,64,640]{2,1,0:T(8,128)(2,1)}, bf16[4,64,640]{2,1,0:T(8,128)(2,1)}, u32[]{:S(2)}, u32[]{:S(2)}) collective-permute-start(bf16[4,64,640]{2,1,0:T(8,128)(2,1)} %get-tuple-element.54), channel_id=1, source_target_pairs={{0,2},{2,0},{1,3},{3,1},{4,6},{6,4},{5,7},{7,5},{8,10},{10,8},{9,1... | collective-permute-start | bytes 983048 | tf_op jit(solution)/shard_map/ppermute | solution.py:38
  79.7 17.5 %collective-permute-start.9 = (bf16[4,64,640]{2,1,0:T(8,128)(2,1)}, bf16[4,64,640]{2,1,0:T(8,128)(2,1)}, u32[]{:S(2)}, u32[]{:S(2)}) collective-permute-start(bf16[4,64,640]{2,1,0:T(8,128)(2,1)} %get-tuple-element.53.refs_0_), channel_id=1, source_target_pairs={{0,4},{4,8},{8,12},{12,0},{1,5},{5,9},{9,13},{13,1},{2,6},{6,10},{... | collective-permute-start | bytes 983048 | tf_op jit(solution)/shard_map/ppermute | solution.py:43
  79.8 22.6 %collective-permute-start.14 = (bf16[4,64,640]{2,1,0:T(8,128)(2,1)}, bf16[4,64,640]{2,1,0:T(8,128)(2,1)}, u32[]{:S(2)}, u32[]{:S(2)}) collective-permute-start(bf16[4,64,640]{2,1,0:T(8,128)(2,1)} %get-tuple-element.54), channel_id=1, source_target_pairs={{0,14},{2,12},{4,2},{6,0},{8,6},{10,4},{12,10},{14,8},{1,15},{3,13... | collective-permute-start | bytes 983048 | tf_op jit(solution)/shard_map/ppermute | solution.py:53
  84.5 17.9 %collective-permute-start.16 = (bf16[4,64,640]{2,1,0:T(8,128)(2,1)}, bf16[4,64,640]{2,1,0:T(8,128)(2,1)}, u32[]{:S(2)}, u32[]{:S(2)}) collective-permute-start(bf16[4,64,640]{2,1,0:T(8,128)(2,1)} %collective-permute-done.8.refs_2_), channel_id=1, source_target_pairs={{0,12},{4,0},{8,4},{12,8},{1,13},{5,1},{9,5},{13,9},{2,14},{6,2},{... | collective-permute-start | bytes 983048 | tf_op jit(solution)/shard_map/ppermute | solution.py:43
  88.5 15.7 %collective-permute-start.17 = (bf16[4,64,640]{2,1,0:T(8,128)(2,1)}, bf16[4,64,640]{2,1,0:T(8,128)(2,1)}, u32[]{:S(2)}, u32[]{:S(2)}) collective-permute-start(bf16[4,64,640]{2,1,0:T(8,128)(2,1)} %collective-permute-done.15.refs_1_), channel_id=1, source_target_pairs={{0,4},{4,8},{8,12},{12,0},{1,5},{5,9},{9,13},{13,1},{2,6},{6,10},{... | collective-permute-start | bytes 983048 | tf_op jit(solution)/shard_map/ppermute | solution.py:43
  110.1 13.7 %collective-permute-start.20 = (bf16[1,80,2432]{2,1,0:T(8,128)(2,1)S(1)}, bf16[1,80,2432]{2,1,0:T(8,128)(2,1)}, u32[]{:S(2)}, u32[]{:S(2)}) collective-permute-start(bf16[1,80,2432]{2,1,0:T(8,128)(2,1)S(1)} %slice.44), channel_id=1, source_target_pairs={{0,12},{4,0},{8,4},{12,8},{1,13},{5,1},{9,5},{13,9},{2,14},{6,2},{... | collective-permute-start | bytes 1167368 | tf_op jit(solution)/shard_map/ppermute | solution.py:43
  111.9 11.8 %collective-permute-start.21 = (bf16[1,80,2432]{2,1,0:T(8,128)(2,1)S(1)}, bf16[1,80,2432]{2,1,0:T(8,128)(2,1)}, u32[]{:S(2)}, u32[]{:S(2)}) collective-permute-start(bf16[1,80,2432]{2,1,0:T(8,128)(2,1)S(1)} %slice.45), channel_id=1, source_target_pairs={{0,4},{4,8},{8,12},{12,0},{1,5},{5,9},{9,13},{13,1},{2,6},{6,10},{... | collective-permute-start | bytes 1167368 | tf_op jit(solution)/shard_map/ppermute | solution.py:43
  111.9 18.4 %collective-permute-start.23 = (bf16[2,80,2432]{2,1,0:T(8,128)(2,1)}, bf16[2,80,2432]{2,1,0:T(8,128)(2,1)}, u32[]{:S(2)}, u32[]{:S(2)}) collective-permute-start(bf16[2,80,2432]{2,1,0:T(8,128)(2,1)} %collective-permute-done.5.refs_1_), channel_id=1, source_target_pairs={{0,1},{1,0},{2,3},{3,2},{4,5},{5,4},{6,7},{7,6},{8,9},{9,8},{10,11... | collective-permute-start | bytes 2334728 | tf_op jit(solution)/shard_map/ppermute | solution.py:38
  112.6 17.8 %collective-permute-start.26 = (bf16[2,80,2432]{2,1,0:T(8,128)(2,1)}, bf16[2,80,2432]{2,1,0:T(8,128)(2,1)}, u32[]{:S(2)}, u32[]{:S(2)}) collective-permute-start(bf16[2,80,2432]{2,1,0:T(8,128)(2,1)} %collective-permute-done.6.refs_4_), channel_id=1, source_target_pairs={{0,1},{1,0},{2,3},{3,2},{4,5},{5,4},{6,7},{7,6},{8,9},{9,8},{10,11... | collective-permute-start | bytes 2334728 | tf_op jit(solution)/shard_map/ppermute | solution.py:38
  112.9 25.3 %collective-permute-start.22 = (bf16[2,80,2432]{2,1,0:T(8,128)(2,1)}, bf16[2,80,2432]{2,1,0:T(8,128)(2,1)}, u32[]{:S(2)}, u32[]{:S(2)}) collective-permute-start(bf16[2,80,2432]{2,1,0:T(8,128)(2,1)} %pad_maximum_fusion.refs_0_), channel_id=1, source_target_pairs={{0,1},{1,0},{2,3},{3,2},{4,5},{5,4},{6,7},{7,6},{8,9},{9,8},{10,11... | collective-permute-start | bytes 2334728 | tf_op jit(solution)/shard_map/ppermute | solution.py:38
  123.8 14.5 %collective-permute-start.24 = (bf16[1,80,2432]{2,1,0:T(8,128)(2,1)}, bf16[1,80,2432]{2,1,0:T(8,128)(2,1)S(1)}, u32[]{:S(2)}, u32[]{:S(2)}) collective-permute-start(bf16[1,80,2432]{2,1,0:T(8,128)(2,1)} %collective-permute-done.20.refs_2_), channel_id=1, source_target_pairs={{0,1},{1,0},{2,3},{3,2},{4,5},{5,4},{6,7},{7,6},{8,9},{9,8},{10,11... | collective-permute-start | bytes 1167368 | tf_op jit(solution)/shard_map/ppermute | solution.py:38
  124.7 13.6 %collective-permute-start.25 = (bf16[1,80,2432]{2,1,0:T(8,128)(2,1)}, bf16[1,80,2432]{2,1,0:T(8,128)(2,1)}, u32[]{:S(2)}, u32[]{:S(2)}) collective-permute-start(bf16[1,80,2432]{2,1,0:T(8,128)(2,1)} %collective-permute-done.21.refs_3_), channel_id=1, source_target_pairs={{0,1},{1,0},{2,3},{3,2},{4,5},{5,4},{6,7},{7,6},{8,9},{9,8},{10,11... | collective-permute-start | bytes 1167368 | tf_op jit(solution)/shard_map/ppermute | solution.py:38
  124.8 13.5 %all-to-all-start.2 = ((bf16[8,64,320]{2,1,0:T(8,128)(2,1)}), bf16[8,64,320]{2,1,0:T(8,128)(2,1)S(1)}, u32[]{:S(2)}, u32[]{:S(2)}) async-start(bf16[8,64,320]{2,1,0:T(8,128)(2,1)} %shard_map.99), calls=%async_computation.2 | async-start | bytes 786432 | tf_op jit(solution)/shard_map/all_to_all | solution.py:400
  (17 other events, 164.1 us)
